TPU v7x, 32 devices: a whole 2x2x4 slice. The times are simulated.
32 devices in a mesh: grp: 4 (over z), dev: 8 (over y, x, core).
Axes of the slice: x: 2, y: 2, z: 4, core: 2. Of those that a mesh axis runs over, the one named last changes fastest.
Arguments:
- inputs: bfloat16 [8, 2048, 1024], P('grp', 'dev'), may hold values from -6 to 6
- cotangent: bfloat16 [8, 2048, 1024], P('grp', 'dev'), may hold values from -6 to 6
- weight_slots: float32 [768, 128, 128], P(('grp', 'dev')), may hold values from -0.1875 to 0.1875
- slot_block: int32 [768], replicated, may hold values from 0 to 767, each once
- left_stats: float32 [768, 128, 128], P(('grp', 'dev')), may hold values from -491.52 to 503316.48, as said below
- right_stats: float32 [768, 128, 128], P(('grp', 'dev')), may hold values from -491.52 to 503316.48, as said below
- left_roots: float32 [768, 128, 128], P(('grp', 'dev')), may hold values from -0.0031570555 to 0.053095133, as said below
- right_roots: float32 [768, 128, 128], P(('grp', 'dev')), may hold values from -0.0031570555 to 0.053095133, as said below
- vectors: float32 [12288], replicated, may hold values from -0.9 to 1.5
- span_start: int32 [8], P('grp'), may hold values from 0 to 1792, as said below
Outputs:
- activations: bfloat16 [8, 2048, 1024], P('grp', 'dev')
- input_grad: float32 [8, 2048, 1024], P('grp', 'dev')
- weight_grads: float32 [768, 128, 128], P(('grp', 'dev'))
- new_left: float32 [768, 128, 128], P(('grp', 'dev'))
- new_right: float32 [768, 128, 128], P(('grp', 'dev'))
- new_weights: float32 [768, 128, 128], P(('grp', 'dev'))
- vector_grads: float32 [12288], replicated
- new_vectors: float32 [12288], replicated
Inputs may be any that keep to these rules, and one draw needn't show every extreme that they name: `slot_block`: each block number once. `span_start`: a multiple of 256; each span lies inside its sequence. `left_stats`: symmetric matrices. `right_stats`: symmetric matrices. `left_roots`: symmetric matrices. `right_roots`: symmetric matrices.
All inputs are finite; a program needn't handle non-finite values.
Results may differ from a plain program's by a relative error of at most 0.012.
Values may be sent and summed in bfloat16 or wider, within the bound.
A program may use at most 320 MiB of HBM per device.

v0:
```python
import functools
import math

import jax
import jax.numpy as jnp
from jax import lax
from jax.experimental import pallas as pl
from jax.experimental.pallas import tpu as pltpu
from jax.sharding import PartitionSpec as P

H = 16
FF = 4096
PIC = 256

eps = 1e-05
weight_rate = 0.5
vector_rate = 0.5
big_negative = -1e30
highest = lax.Precision.HIGHEST
F32 = jnp.float32
BF16 = jnp.bfloat16
LOG2E = 1.4426950408889634
MIB = 1024 * 1024

GAIN1, SHIFT1, BQ, BV, BO, GAIN2, SHIFT2, BDOWN, BUP = range(9)


def dot_nn(a, b):
    return lax.dot_general(a, b, (((1,), (0,)), ((), ())), preferred_element_type=F32)


def dot_nt(a, b):
    return lax.dot_general(a, b, (((1,), (1,)), ((), ())), preferred_element_type=F32)


def turn(v):
    return v.astype(F32).T.astype(BF16)


def vmem():
    return pl.BlockSpec(memory_space=pltpu.VMEM)


def smem():
    return pl.BlockSpec(memory_space=pltpu.SMEM)


def hbm():
    return pl.BlockSpec(memory_space=pl.ANY)


def sds(shape, dtype):
    return jax.ShapeDtypeStruct(shape, dtype)


def params(mib=58, **kw):
    return pltpu.CompilerParams(vmem_limit_bytes=mib * MIB, **kw)


def layer_stats(v):
    middle = jnp.mean(v, axis=-1, keepdims=True)
    centred = v - middle
    spread = jnp.mean(centred * centred, axis=-1, keepdims=True)
    return centred, lax.rsqrt(spread + eps)


def fold_rows(v):
    return jnp.sum(v.reshape(v.shape[0] // 8, 8, v.shape[1]), axis=0)


def slot_at(slot_ref, block):
    lanes = slot_ref.shape[1]
    if isinstance(block, int):
        return slot_ref[block // lanes, block % lanes]
    return slot_ref[lax.div(block, lanes), lax.rem(block, lanes)]


def fetch_block(gath, slot, dst, row, col, sem, side):
    return pltpu.make_async_copy(
        gath.at[slot], dst.at[pl.ds(row, side), pl.ds(col, side)], sem
    )


def prepare(x_ref, block_ref, vin_ref, h1_ref, slot_ref, vec_ref):
    rows, width = x_ref.shape
    per = width // 128
    for r in range(vec_ref.shape[0]):
        for c in range(per):
            vec_ref[r:r + 1, c * 128:(c + 1) * 128] = vin_ref[per * r + c:per * r + c + 1, :]
    chunk = 128

    @pl.loop(0, rows // chunk)
    def _(r):
        at = pl.ds(pl.multiple_of(r * chunk, chunk), chunk)
        centred, inv = layer_stats(x_ref[at, :].astype(F32))
        h1_ref[at, :] = (
            centred * inv * vec_ref[GAIN1:GAIN1 + 1, :] + vec_ref[SHIFT1:SHIFT1 + 1, :]
        ).astype(BF16)

    tiles, lanes = slot_ref.shape
    line = lax.broadcasted_iota(jnp.int32, (8, lanes), 0)
    lane = lax.broadcasted_iota(jnp.int32, (8, lanes), 1).astype(F32)
    block = lax.broadcasted_iota(jnp.int32, (lanes, lanes), 0)
    for t in range(tiles):
        found = jnp.zeros((8, lanes), F32)
        for r in range(tiles):
            held = (block_ref[r:r + 1, :] == block + t * lanes).astype(F32).astype(BF16)
            found = found + dot_nt(jnp.where(line == 0, lane, float(r)).astype(BF16), held)
        slot_ref[t:t + 1, :] = (found[0:1] + float(lanes) * found[1:2]).astype(jnp.int32)


def prepared_shapes(x, blocks, vin):
    rows, width = x.shape
    return (
        sds((rows, width), BF16),
        sds(blocks.shape, jnp.int32),
        sds((vin.size // width, width), F32),
    )


def run_prepare(x, blocks, vin):
    return pl.pallas_call(
        prepare,
        out_shape=prepared_shapes(x, blocks, vin),
        in_specs=[vmem()] * 3,
        out_specs=tuple([vmem()] * 3),
        compiler_params=params(),
        name="prepare",
    )(x, blocks, vin)


def qkv_kernel(slot_ref, h1_ref, vec_ref, gath, out_ref, wq_out, wbuf, sems, sem_w, *, nd):
    rows, width = h1_ref.shape
    side = gath.shape[1]
    per = width // side
    lanes = out_ref.shape[3]
    for part in range(3):
        for i in range(per):
            for j in range(per):
                slot = slot_at(slot_ref, i * 3 * per + part * per + j)
                fetch_block(gath, slot, wbuf.at[part], i * side, j * side, sems.at[part], side).start()

    def keep(part):
        return pltpu.make_async_copy(wbuf.at[part], wq_out.at[part], sem_w.at[part])

    for part in range(3):
        pltpu.make_async_copy(wbuf.at[part], wbuf.at[part], sems.at[part]).wait()
        keep(part).start()
        for half in range(2):
            cols = slice(half * width // 2, (half + 1) * width // 2)
            res = dot_nn(h1_ref[...], wbuf[part, :, cols])
            if part == 0:
                res = res + vec_ref[BQ:BQ + 1, cols]
            if part == 2:
                res = res + vec_ref[BV:BV + 1, cols]
            res = res.astype(BF16)
            for d in range(nd // 2):
                out_ref[half * (nd // 2) + d, part, :, :] = res[:, d * lanes:(d + 1) * lanes]
    for part in range(3):
        keep(part).wait()


def run_qkv(slot_of, h1, vec, gath, nd):
    rows, width = h1.shape
    lanes = width // nd
    return pl.pallas_call(
        functools.partial(qkv_kernel, nd=nd),
        out_shape=(sds((nd, 3, rows, lanes), BF16), sds((3, width, width), BF16)),
        in_specs=[smem(), vmem(), vmem(), hbm()],
        out_specs=(vmem(), hbm()),
        scratch_shapes=[
            pltpu.VMEM((3, width, width), BF16),
            pltpu.SemaphoreType.DMA((3,)),
            pltpu.SemaphoreType.DMA((3,)),
        ],
        compiler_params=params(),
        name="qkv",
    )(slot_of, h1, vec, gath)


MESH = pl.DeviceIdType.MESH


def remote(src, dst, send, recv, device):
    return pltpu.make_async_remote_copy(
        src_ref=src, dst_ref=dst, send_sem=send, recv_sem=recv, device_id=device, device_id_type=MESH
    )


def arrived(ref, sem):
    pltpu.make_async_copy(ref, ref, sem).wait()


def cut(ref, first, size):
    return ref.at[pl.ds(first, size)]


def greet_plane(g, d, nd):
    barrier = pltpu.get_barrier_semaphore()
    for p in range(1, nd):
        pl.semaphore_signal(barrier, inc=1, device_id=(g, lax.rem(d + p, nd)), device_id_type=MESH)
    pl.semaphore_wait(barrier, nd - 1)


def landing(ref, part, source, q, tok, lanes, parts):
    if lanes % 128 == 0:
        first = (part * (ref.shape[1] // parts)) + source * lanes
        return ref.at[pl.ds(q * tok, tok), pl.ds(pl.multiple_of(first, lanes), lanes)]
    return ref.at[source, part, q]


def landing_shape(parts, nb, seqs, tok, lanes):
    if lanes % 128 == 0:
        return sds((seqs * tok, parts * nb * lanes), BF16)
    return sds((nb, parts, seqs, tok, lanes), BF16)


def side_by_side(got, parts, rows):
    if got.ndim == 2:
        return got
    nb, _, seqs, tok, lanes = got.shape
    return got.transpose(2, 3, 1, 0, 4).reshape(rows, parts * nb * lanes)


def parts3(v):
    hi = v.astype(BF16)
    mid = (v - hi.astype(F32)).astype(BF16)
    lo = (v - hi.astype(F32) - mid.astype(F32)).astype(BF16)
    return hi.astype(F32), mid.astype(F32), lo.astype(F32)


def own_lanes(h, shape, hpd, lanes):
    lane = lax.broadcasted_iota(jnp.int32, shape, 1)
    size = lanes // hpd
    return (lane >= h * size) & (lane < (h + 1) * size)


def place(values, base, tok, width):
    lane = lax.broadcasted_iota(jnp.int32, (tok, width), 1)
    out = jnp.zeros((tok, width), F32)
    for n, v in enumerate(values):
        out = jnp.where(lane == base + n, v, out)
    return out


def spare(h, hpd, lanes):
    return (lanes // hpd) * (1 - h) if hpd > 1 else 0


def column_tables(slope_ref, qbase, kbase, kfar, hpd, lanes):
    _, tok, _ = qbase.shape
    u = lax.broadcasted_iota(jnp.int32, (tok, 128), 0).astype(F32)
    for h in range(hpd):
        slope = slope_ref[h] * LOG2E
        base = spare(h, hpd, lanes)
        near = parts3(jnp.full((tok, 128), slope, F32))
        far = parts3(jnp.full((tok, 128), slope * tok, F32))
        qbase[h] = place(near + far, base, tok, 128)
        kbase[h] = place([u] * 3 + [0.0] * 3 + [1.0] * 3, base, tok, 128)
        kfar[h] = place([0.0] * 3 + [1.0] * 3, base, tok, 128)


def extra_lanes(columns, extra, h, hpd, lanes):
    lane = lax.broadcasted_iota(jnp.int32, columns.shape, 1)
    for n, v in enumerate(extra):
        columns = jnp.where(lane == spare(h, hpd, lanes) + 6 + n, v, columns)
    return columns


def q_columns(q, h, hpd, columns, extra):
    tok, lanes = q.shape
    scaled = q.astype(F32) * ((lanes // hpd) ** (-0.5) * LOG2E)
    hi = scaled.astype(BF16).astype(F32)
    low = scaled - hi
    if extra:
        columns = extra_lanes(columns, extra, h, hpd, lanes)
    if hpd > 1:
        own = own_lanes(h, (tok, lanes), hpd, lanes)
        return jnp.concatenate(
            [jnp.where(own, hi, 0.0), jnp.where(own, low, columns)], axis=1
        ).astype(BF16)
    return jnp.concatenate([hi, low, columns], axis=1).astype(BF16)


def k_columns(k, h, hpd, columns):
    tok, lanes = k.shape
    wide = k.astype(F32)
    if hpd > 1:
        own = own_lanes(h, (tok, lanes), hpd, lanes)
        return jnp.concatenate([wide, jnp.where(own, wide, columns)], axis=1).astype(BF16)
    return jnp.concatenate([wide, wide, columns], axis=1).astype(BF16)


def far_side(slope, tok):
    u = lax.broadcasted_iota(jnp.int32, (tok, tok), 0)
    t = lax.broadcasted_iota(jnp.int32, (tok, tok), 1)
    after = u > t
    return (
        jnp.where(after, big_negative, 0.0),
        jnp.where(after, (2.0 * slope) * (t - u).astype(F32), 0.0),
    )


def pair_tables(corr, h, mask, span):
    tok = mask.shape[0]
    for n, (one, two) in enumerate(((mask, mask), (span, mask), (mask, span))):
        corr[h, n, 0:tok, 0:tok] = one
        corr[h, n, tok:, tok:] = two
        corr[h, n, 0:tok, tok:] = jnp.zeros((tok, tok), F32)
        corr[h, n, tok:, 0:tok] = jnp.full((tok, tok), big_negative, F32)


def attn_fwd_kernel(
    span_ref, slope_ref, src, got_out, o_got, o32_out, lse_out,
    got, o32_ref, lse_ref, sem_w, qa, ka, vt, scores, weights, tops_ref, corr, qbase, kbase, kfar, o_out, ss, sr, os, orr, loc, *, hpd, nd
):
    nb, _, seqs, tok, lanes = got.shape
    size = lanes // hpd
    pair = 2 * tok
    strip = 32
    g = lax.axis_index("grp")
    d = lax.axis_index("dev")

    for q in range(seqs):
        pltpu.make_async_copy(src.at[d, :, q], got.at[d, :, q], loc.at[q]).start()
    greet_plane(g, d, nd)

    def kind_of(kind):
        return pl.ds(2 * kind, 2 - kind)

    def send(q, kind, p):
        to = lax.rem(d + p, nd)
        return remote(
            src.at[to, kind_of(kind), q], got.at[d, kind_of(kind), q],
            ss.at[q, kind, p], sr.at[q, kind, p], (g, to),
        )

    def send_all(q, kind):
        @pl.loop(1, nd)
        def _(p):
            send(q, kind, p).start()

    def have(q, kind):
        @pl.loop(1, nd)
        def _(p):
            arrived(got.at[lax.rem(d + nd - p, nd), kind_of(kind), q], sr.at[q, kind, p])

    send_all(0, 0)
    send_all(0, 1)

    def o_place(source, q):
        return landing(o_got, 0, source, q, tok, lanes, 1)

    def send_o(q, i, p):
        return remote(o_out.at[i, q], o_place(d, q), os.at[q, i], orr.at[q, p], (g, i))

    column_tables(slope_ref, qbase, kbase, kfar, hpd, lanes)
    for h in range(hpd):
        mask, span = far_side(slope_ref[h] * LOG2E, tok)
        pair_tables(corr, h, mask, span)

    def fold(v, how):
        return how(v.reshape(v.shape[0] // 8, 8, v.shape[1]), axis=0)

    def write(ref, out, n, q, third=False):
        if third:
            return pltpu.make_async_copy(ref.at[:, :, q], out.at[:, :, q], sem_w.at[n, q])
        return pltpu.make_async_copy(ref.at[:, q], out.at[:, q], sem_w.at[n, q])

    whole = scores.shape[1] > nb // 2

    def tile_at(i, n):
        return (i * (i + 1)) // 2 + n if whole else n

    @pl.loop(0, seqs)
    def _(q):
        pltpu.make_async_copy(src.at[d, :, q], got.at[d, :, q], loc.at[q]).wait()
        start = span_ref[q]

        def score(i):
            flag = (start == i * pair).astype(jnp.int32) + 2 * (start == i * pair + tok).astype(jnp.int32)
            at_i = slice(i * pair, (i + 1) * pair)
            for h in range(hpd):
                top = None
                for n in range(i + 1):
                    at = tile_at(i, n)
                    scores[h, at] = dot_nt(ka[h, n * pair:(n + 1) * pair, :], qa[h, at_i, :])
                    for r in range(0, pair, strip):
                        rows = slice(r, r + strip)
                        v = scores[h, at, rows, :]
                        if n == i:
                            v = v + corr[h, flag, rows, :]
                            scores[h, at, rows, :] = v
                        here = fold(v, jnp.max)
                        top = here if top is None else jnp.maximum(top, here)
                tops_ref[h, i] = jnp.broadcast_to(jnp.max(top, axis=0, keepdims=True), (8, pair))

        have(q, 0)

        @pl.when(q + 1 < seqs)
        def _():
            send_all(q + 1, 0)

        @pl.loop(0, nb)
        def _(j):
            at_j = pl.ds(pl.multiple_of(j * tok, tok), tok)
            block = jnp.full((tok, 128), j, jnp.int32).astype(F32)
            for h in range(hpd):
                qa[h, at_j, :] = q_columns(got[j, 0, q], h, hpd, qbase[h], [])
                ka[h, at_j, :] = k_columns(got[j, 1, q], h, hpd, kbase[h] + block * kfar[h])

        if whole:
            for i in range(nb // 2):
                score(i)
        have(q, 1)

        @pl.when(q + 1 < seqs)
        def _():
            send_all(q + 1, 1)

        write(got, got_out, 0, q, True).start()

        @pl.loop(0, nb)
        def _(j):
            vt[0:lanes, pl.ds(pl.multiple_of(j * tok, tok), tok)] = turn(got[j, 2, q])

        for i in range(nb // 2):
            if not whole:
                score(i)
            outs = []
            logs = []
            for h in range(hpd):
                acc = total = None
                top = tops_ref[h, i][0:1]
                for n in range(i + 1):
                    at = tile_at(i, n)
                    for r in range(0, pair, strip):
                        rows = slice(r, r + strip)
                        p = jnp.exp2(scores[h, at, rows, :] - top)
                        here = fold(p, jnp.sum)
                        total = here if total is None else total + here
                        weights[h, n % 2, rows, :] = p.astype(BF16)
                    part = dot_nn(vt[h * size:(h + 1) * size, n * pair:(n + 1) * pair], weights[h, n % 2])
                    acc = part if acc is None else acc + part
                total = jnp.sum(total, axis=0, keepdims=True)
                outs.append(acc / total)
                logs.append(jnp.broadcast_to(top + jnp.log2(total), (128 // hpd, pair)))
            out = (jnp.concatenate(outs, axis=0) if hpd > 1 else outs[0]).T
            log = (jnp.concatenate(logs[::-1], axis=0) if hpd > 1 else logs[0]).T
            for k in range(2):
                at = 2 * i + k
                o32_ref[at, q] = out[k * tok:(k + 1) * tok]
                o_out[at, q] = out[k * tok:(k + 1) * tok].astype(BF16)
                lse_ref[at, q] = log[k * tok:(k + 1) * tok]

                @pl.when(at == d)
                def _():
                    pltpu.make_async_copy(o_out.at[at, q], o_place(d, q), os.at[q, at]).start()

                @pl.when(at != d)
                def _():
                    send_o(q, at, lax.rem(at - d + nd, nd)).start()

        write(o32_ref, o32_out, 1, q).start()
        write(lse_ref, lse_out, 2, q).start()

    for q in range(seqs):
        @pl.loop(1, nd)
        def _(p):
            arrived(o_place(lax.rem(d + nd - p, nd), q), orr.at[q, p])
            send(q, 0, p).wait_send()
            send(q, 1, p).wait_send()

        @pl.loop(0, nd)
        def _(i):
            arrived(o_out.at[i, q], os.at[q, i])
        write(got, got_out, 0, q, True).wait()
        write(o32_ref, o32_out, 1, q).wait()
        write(lse_ref, lse_out, 2, q).wait()


def run_attn_fwd(span, slopes, qkv, hpd):
    nb, _, seqs, tok, lanes = qkv.shape
    t = nb * tok
    pairs = nb // 2
    tiles = pairs * (pairs + 1) // 2
    if hpd * tiles > 24:
        tiles = pairs
    dma = pltpu.SemaphoreType.DMA
    return pl.pallas_call(
        functools.partial(attn_fwd_kernel, hpd=hpd, nd=nb),
        out_shape=(
            sds(qkv.shape, BF16),
            landing_shape(1, nb, seqs, tok, lanes),
            sds((nb, seqs, tok, lanes), F32),
            sds((nb, seqs, tok, 128), F32),
        ),
        in_specs=[smem(), smem(), hbm()],
        out_specs=(hbm(), vmem(), hbm(), hbm()),
        scratch_shapes=[
            pltpu.VMEM(qkv.shape, BF16),
            pltpu.VMEM((nb, seqs, tok, lanes), F32),
            pltpu.VMEM((nb, seqs, tok, 128), F32),
            dma((3, seqs)),
            pltpu.VMEM((hpd, t, 256), BF16),
            pltpu.VMEM((hpd, t, 256), BF16),
            pltpu.VMEM((lanes, t), BF16),
            pltpu.VMEM((hpd, tiles, 2 * tok, 2 * tok), F32),
            pltpu.VMEM((hpd, 2, 2 * tok, 2 * tok), BF16),
            pltpu.VMEM((hpd, nb // 2, 8, 2 * tok), F32),
            pltpu.VMEM((hpd, 3, 2 * tok, 2 * tok), F32),
            pltpu.VMEM((hpd, tok, 128), F32),
            pltpu.VMEM((hpd, tok, 128), F32),
            pltpu.VMEM((hpd, tok, 128), F32),
            pltpu.VMEM((nb, seqs, tok, lanes), BF16),
            dma((seqs, 2, nb)),
            dma((seqs, 2, nb)),
            dma((seqs, nb)),
            dma((seqs, nb)),
            dma((seqs,)),
        ],
        compiler_params=params(collective_id=2, has_side_effects=True),
        name="attn_fwd",
    )(span, slopes, qkv)


def attn_bwd_kernel(
    span_ref, slope_ref, qkv_in, do_src, o32_in, lse_in, got,
    qkv_ref, o32_ref, lse_ref, sem_in, do_got, out, qa, ka, kt, va, qm, da, dm, dqt, corr, qbase, kbase, kfar,
    s_ref, dp_ref, p_ref, ds_ref, ss, sr, gs, gr, loc, *, hpd, nd
):
    nb, _, seqs, tok, lanes = qkv_ref.shape
    inputs = [
        pltpu.make_async_copy(qkv_in, qkv_ref, sem_in.at[0]),
        pltpu.make_async_copy(lse_in, lse_ref, sem_in.at[1]),
        pltpu.make_async_copy(o32_in, o32_ref, sem_in.at[2]),
    ]
    for copy in inputs:
        copy.start()
    size = lanes // hpd
    unit = size ** (-0.5)
    pair = 2 * tok
    strip = 32
    g = lax.axis_index("grp")
    d = lax.axis_index("dev")

    def own_copy(q):
        return pltpu.make_async_copy(do_src.at[d, q], do_got.at[d, q], loc.at[q])

    for q in range(seqs):
        own_copy(q).start()
    greet_plane(g, d, nd)

    def send(q, p):
        to = lax.rem(d + p, nd)
        return remote(do_src.at[to, q], do_got.at[d, q], ss.at[q, p], sr.at[q, p], (g, to))

    def send_all(q):
        @pl.loop(1, nd)
        def _(p):
            send(q, p).start()

    send_all(0)

    def place_back(kind, source, q):
        return landing(got, kind, source, q, tok, lanes, 3)

    def back(q, kind, p):
        to = lax.rem(d + p, nd)
        return remote(
            out.at[to, kind, q], place_back(kind, d, q), gs.at[q, kind, p], gr.at[q, kind, p], (g, to)
        )

    def back_own(q, kind):
        return pltpu.make_async_copy(out.at[d, kind, q], place_back(kind, d, q), gs.at[q, kind, 0])

    for h in range(hpd):
        mask, span = far_side(slope_ref[h] * LOG2E, tok)
        pair_tables(corr, h, mask, span)
    column_tables(slope_ref, qbase, kbase, kfar, hpd, lanes)
    row = lax.broadcasted_iota(jnp.int32, (lanes, lanes), 0) // size
    col = lax.broadcasted_iota(jnp.int32, (lanes, lanes), 1) // size
    across = (row == hpd - 1 - col).astype(F32).astype(BF16)
    for copy in inputs:
        copy.wait()

    @pl.loop(0, seqs)
    def _(q):
        @pl.loop(0, nb)
        def _(j):
            at_j = pl.ds(pl.multiple_of(j * tok, tok), tok)
            qj = qkv_ref[j, 0, q]
            kj = qkv_ref[j, 1, q]
            vj = qkv_ref[j, 2, q].astype(F32)
            kt[:, at_j] = kj.astype(F32).T.astype(BF16)
            dqt[:, at_j] = jnp.zeros((lanes, tok), F32)
            block = jnp.full((tok, 128), j, jnp.int32).astype(F32)
            low = [-p for p in parts3(lse_ref[j, q])]
            for h in range(hpd):
                qa[h, at_j, :] = q_columns(qj, h, hpd, qbase[h], low)
                ka[h, at_j, :] = k_columns(kj, h, hpd, kbase[h] + block * kfar[h])
                if hpd > 1:
                    own = own_lanes(h, (tok, lanes), hpd, lanes)
                    qm[h, at_j, :] = jnp.where(own, qj.astype(F32), 0.0).astype(BF16)
                    va[h, at_j, :] = jnp.where(own, vj, kbase[h]).astype(BF16)
                else:
                    qm[h, at_j, :] = qj
                    va[h, at_j, :] = jnp.concatenate([vj, kbase[h][:, 0:lanes]], axis=1).astype(BF16)

        own_copy(q).wait()

        @pl.loop(1, nd)
        def _(p):
            arrived(do_got.at[lax.rem(d + nd - p, nd), q], sr.at[q, p])

        @pl.when(q + 1 < seqs)
        def _():
            send_all(q + 1)

        @pl.loop(0, nb)
        def _(j):
            at_j = pl.ds(pl.multiple_of(j * tok, tok), tok)
            do = do_got[j, q].astype(F32)
            delta = jnp.zeros((tok, lanes), F32)
            for p in parts3(do * o32_ref[j, q]):
                delta = delta + dot_nn(p.astype(BF16), across)
            low = [-p for p in parts3(delta)]
            for h in range(hpd):
                if hpd > 1:
                    own = own_lanes(h, (tok, lanes), hpd, lanes)
                    none = jnp.where(own, do, 0.0)
                    da[h, at_j, :] = extra_lanes(none, low, h, hpd, lanes).astype(BF16)
                    dm[h, at_j, :] = none.astype(BF16)
                else:
                    extra = extra_lanes(jnp.zeros((tok, lanes), F32), low, h, hpd, lanes)
                    da[h, at_j, :] = jnp.concatenate([do, extra], axis=1).astype(BF16)
                    dm[h, at_j, :] = do.astype(BF16)

        start = span_ref[q]

        pairs = nb // 2

        def tile(j, i):
            at_j = slice(j * pair, (j + 1) * pair)
            at_i = slice(i * pair, (i + 1) * pair)
            flag = (start == j * pair).astype(jnp.int32) + 2 * (start == j * pair + tok).astype(jnp.int32)
            dk = dv = None
            for h in range(hpd):
                s_ref[h] = dot_nt(ka[h, at_j, :], qa[h, at_i, :])
                dp_ref[h] = dot_nt(va[h, at_j, :], da[h, at_i, :])
                for r in range(0, pair, strip):
                    rows = slice(r, r + strip)
                    s = s_ref[h, rows, :]
                    if i == j:
                        s = s + corr[h, flag, rows, :]
                    p = jnp.exp2(s)
                    p_ref[h, rows, :] = p.astype(BF16)
                    ds_ref[h, rows, :] = (p * dp_ref[h, rows, :]).astype(BF16)
                ds = ds_ref[h]
                dv_h = dot_nn(p_ref[h], dm[h, at_i, :])
                dk_h = dot_nn(ds, qm[h, at_i, :])
                dk = dk_h if dk is None else dk + dk_h
                dv = dv_h if dv is None else dv + dv_h
                rows = slice(h * size, (h + 1) * size)
                dqt[rows, at_i] += dot_nn(kt[rows, at_j], ds)
            return dk, dv

        @pl.loop(0, pairs)
        def _(n):
            turn_of = lax.rem(d // 2 + n, pairs)
            for case in range(pairs):
                @pl.when(turn_of == case)
                def _():
                    dk, dv = tile(case, case)
                    for i in range(case + 1, pairs):
                        more = tile(case, i)
                        dk = dk + more[0]
                        dv = dv + more[1]
                    for k in range(2):
                        half = slice(k * tok, (k + 1) * tok)
                        out[2 * case + k, 1, q] = (dk[half] * unit).astype(BF16)
                        out[2 * case + k, 2, q] = dv[half].astype(BF16)

            for k in range(2):
                j = 2 * turn_of + k
                for kind in (1, 2):
                    @pl.when(j == d)
                    def _():
                        back_own(q, kind).start()

                    @pl.when(j != d)
                    def _():
                        back(q, kind, lax.rem(j - d + nd, nd)).start()

        @pl.loop(0, nb)
        def _(n):
            j = lax.rem(d + n, nb)
            at_j = pl.ds(pl.multiple_of(j * tok, tok), tok)
            out[j, 0, q] = (dqt[:, at_j].T * unit).astype(BF16)

            @pl.when(n == 0)
            def _():
                back_own(q, 0).start()

            @pl.when(n > 0)
            def _():
                back(q, 0, n).start()

    for q in range(seqs):
        for kind in range(3):
            back_own(q, kind).wait()

        @pl.loop(1, nd)
        def _(p):
            send(q, p).wait_send()
            source = lax.rem(d + nd - p, nd)
            for kind in range(3):
                back(q, kind, p).wait_send()
                arrived(place_back(kind, source, q), gr.at[q, kind, p])


def run_attn_bwd(span, slopes, qkv, do, o32, lse, hpd):
    nb, _, seqs, tok, lanes = qkv.shape
    t = nb * tok
    dma = pltpu.SemaphoreType.DMA
    wide = 128 if hpd == 1 else lanes
    return pl.pallas_call(
        functools.partial(attn_bwd_kernel, hpd=hpd, nd=nb),
        out_shape=landing_shape(3, nb, seqs, tok, lanes),
        in_specs=[smem(), smem(), hbm(), hbm(), hbm(), hbm()],
        out_specs=vmem(),
        scratch_shapes=[
            pltpu.VMEM(qkv.shape, BF16),
            pltpu.VMEM(o32.shape, F32),
            pltpu.VMEM(lse.shape, F32),
            dma((3,)),
            pltpu.VMEM((nb, seqs, tok, lanes), BF16),
            pltpu.VMEM(qkv.shape, BF16),
            pltpu.VMEM((hpd, t, 256), BF16),
            pltpu.VMEM((hpd, t, 256), BF16),
            pltpu.VMEM((lanes, t), BF16),
            pltpu.VMEM((hpd, t, wide), BF16),
            pltpu.VMEM((hpd, t, lanes), BF16),
            pltpu.VMEM((hpd, t, wide), BF16),
            pltpu.VMEM((hpd, t, lanes), BF16),
            pltpu.VMEM((lanes, t), F32),
            pltpu.VMEM((hpd, 3, 2 * tok, 2 * tok), F32),
            pltpu.VMEM((hpd, tok, 128), F32),
            pltpu.VMEM((hpd, tok, 128), F32),
            pltpu.VMEM((hpd, tok, 128), F32),
            pltpu.VMEM((hpd, 2 * tok, 2 * tok), F32),
            pltpu.VMEM((hpd, 2 * tok, 2 * tok), F32),
            pltpu.VMEM((hpd, 2 * tok, 2 * tok), BF16),
            pltpu.VMEM((hpd, 2 * tok, 2 * tok), BF16),
            dma((seqs, nb)),
            dma((seqs, nb)),
            dma((seqs, 3, nb)),
            dma((seqs, 3, nb)),
            dma((seqs,)),
        ],
        compiler_params=params(collective_id=3, has_side_effects=True),
        name="attn_bwd",
    )(span, slopes, qkv, do, o32, lse)


def mlp_kernel(
    slot_ref, att_in, x_in, dy_in, vec_ref, gath,
    act_out, dx1_out, do_out, sums_ref, grads,
    att_ref, x_ref, dy_ref, sem_in, wo, wup, wdn, x1, acc, dh2, h2_ref, h2t, attt, act_ref, z_ref, dg_ref, g_ref, dz_ref, do_ref, stage,
    sem_o, sem_t, sem_g, sem_w, *, nd, first_o, first_up, first_dn, tile
):
    rows, width = x_ref.shape
    side = gath.shape[1]
    per = width // side
    ff = sums_ref.shape[0] // 8 * width - 4 * width
    tiles = ff // tile
    cols = tile // side
    lanes = do_ref.shape[2]
    fper = ff // side
    inputs = [
        pltpu.make_async_copy(att_in, att_ref, sem_in.at[0]),
        pltpu.make_async_copy(x_in, x_ref, sem_in.at[1]),
        pltpu.make_async_copy(dy_in, dy_ref, sem_in.at[2]),
    ]
    for copy in inputs:
        copy.start()

    for i in range(per):
        for j in range(per):
            fetch_block(gath, slot_at(slot_ref, first_o + i * per + j), wo, i * side, j * side, sem_o.at[0], side).start()

    ring = wup.shape[0]

    def fetch_tile(f):
        at = f % ring
        for i in range(per):
            for j in range(cols):
                fetch_block(gath, slot_at(slot_ref, first_up + i * fper + f * cols + j), wup.at[at], i * side, j * side, sem_t.at[at], side).start()
            for j in range(cols):
                fetch_block(gath, slot_at(slot_ref, first_dn + (f * cols + j) * per + i), wdn.at[at], j * side, i * side, sem_t.at[at], side).start()

    for f in range(min(ring, tiles)):
        fetch_tile(f)
    for copy in inputs:
        copy.wait()
    for r in range(width // 256):
        attt[r * 256:(r + 1) * 256, :] = turn(att_ref[:, r * 256:(r + 1) * 256])
    pltpu.make_async_copy(wo, wo, sem_o.at[0]).wait()
    for half in range(2):
        c = slice(half * width // 2, (half + 1) * width // 2)
        x1[:, c] = x_ref[:, c].astype(F32) + dot_nn(att_ref[...], wo[:, c]) + vec_ref[BO:BO + 1, c]

    chunk = 128

    def rows_at(r):
        return pl.ds(pl.multiple_of(r * chunk, chunk), chunk)

    @pl.loop(0, rows // chunk)
    def _(r):
        at = rows_at(r)
        centred, inv = layer_stats(x1[at, :])
        h2_ref[at, :] = (centred * inv * vec_ref[GAIN2:GAIN2 + 1, :] + vec_ref[SHIFT2:SHIFT2 + 1, :]).astype(BF16)
        acc[at, :] = x1[at, :] + vec_ref[BDOWN:BDOWN + 1, :]
        dh2[at, :] = jnp.zeros((chunk, width), F32)

    for r in range(width // 256):
        h2t[r * 256:(r + 1) * 256, :] = turn(h2_ref[:, r * 256:(r + 1) * 256])

    def put(slot, first, res, down, across):
        for i in range(down):
            for j in range(across):
                stage[slot, first + i * across + j] = res[i * side:(i + 1) * side, j * side:(j + 1) * side]

    def leave(slot, n, block):
        pltpu.make_async_copy(stage.at[slot, n], grads.at[slot_at(slot_ref, block)], sem_g.at[slot]).start()

    def left(slot, size):
        at = stage.at[slot, pl.ds(0, size)]
        pltpu.make_async_copy(at, at, sem_g.at[slot]).wait()

    full = 2 * per * cols
    piece = 512
    per_piece = piece // side
    strip = 16

    def pieces(size):
        return [slice(k * piece, (k + 1) * piece) for k in range(size // piece)]

    def into_tile(f):
        at = f % ring
        arrived(wup.at[at], sem_t.at[at])
        arrived(wdn.at[at], sem_t.at[at])
        for c in pieces(tile):
            z_ref[:, c] = dot_nn(h2_ref[...], wup[at, :, c])
            dg_ref[:, c] = dot_nt(dy_ref[...], wdn[at, c, :])

    def gelu_strips(f, first, last):
        total = None
        for r in range(first, last, strip):
            at = slice(r, r + strip)
            z = z_ref[at, :] + vec_ref[BUP + f:BUP + f + 1, :]
            z2 = z * z
            th = jnp.tanh(z * (0.7978845608028654 + (0.7978845608028654 * 0.044715) * z2))
            half_more = 0.5 + 0.5 * th
            g_ref[f % 2, at, :] = (z * half_more).astype(BF16)
            slope = half_more + (0.5 * z) * (1.0 - th * th) * (
                0.7978845608028654 + (3.0 * 0.044715 * 0.7978845608028654) * z2
            )
            dz = (dg_ref[at, :] * slope).astype(BF16)
            dz_ref[f % 2, at, :] = dz
            here = fold_rows(dz.astype(F32))
            total = here if total is None else total + here
        at = slice(8 * (4 + f), 8 * (4 + f) + 8)
        if first == 0:
            sums_ref[at, :] = total
        else:
            sums_ref[at, :] += total

    def out_of_tile(f):
        at = f % ring
        slot = f % 2

        def up(c):
            acc[:, c] += dot_nn(g_ref[slot], wdn[at, :, c])
            dh2[:, c] += dot_nt(dz_ref[slot], wup[at, c, :])

        def grad_down(k, c):
            res = dot_nn(turn(g_ref[slot, :, c]), dy_ref[...]).astype(BF16)
            put(slot, k * per_piece * per, res, per_piece, per)

        def grad_up(k, c):
            res = dot_nn(h2t[c, :], dz_ref[slot]).astype(BF16)
            put(slot, per * cols + k * per_piece * cols, res, per_piece, cols)

        steps = [functools.partial(up, c) for c in pieces(width)]
        steps += [functools.partial(grad_down, k, c) for k, c in enumerate(pieces(tile))]
        steps += [functools.partial(grad_up, k, c) for k, c in enumerate(pieces(width))]
        return steps

    def send_tile(f):
        slot = f % 2
        for i in range(per):
            for j in range(cols):
                leave(slot, j * per + i, first_dn + (f * cols + j) * per + i)
            for j in range(cols):
                leave(slot, per * cols + i * cols + j, first_up + i * fper + f * cols + j)

    for f in range(tiles + 1):
        if f < tiles:
            into_tile(f)
        steps = out_of_tile(f - 1) if f > 0 else []
        if f > 2:
            left((f - 1) % 2, full)
        share = rows // max(len(steps), 1)
        if f < tiles:
            for n in range(max(len(steps), 1)):
                gelu_strips(f, n * share // strip * strip, rows if n + 1 >= len(steps) else (n + 1) * share // strip * strip)
                if steps:
                    steps[n]()
        else:
            for step in steps:
                step()
        if f > 0:
            send_tile(f - 1)
            if f - 1 + ring < tiles:
                fetch_tile(f - 1 + ring)

    zero = jnp.zeros((8, width), F32)
    da_ref = h2_ref
    dx1_ref = x1

    def finish(r, carry):
        s_bo, s_gain, s_shift, s_bdown = carry
        at = rows_at(r)
        act_ref[at, :] = acc[at, :].astype(BF16)
        centred, inv = layer_stats(x1[at, :])
        hat = centred * inv
        dh = dh2[at, :]
        dhg = dh * vec_ref[GAIN2:GAIN2 + 1, :]
        back = inv * (
            dhg
            - jnp.mean(dhg, axis=-1, keepdims=True)
            - hat * jnp.mean(dhg * hat, axis=-1, keepdims=True)
        )
        dy = dy_ref[at, :].astype(F32)
        dx1 = dy + back
        dx1_ref[at, :] = dx1
        da = dx1.astype(BF16)
        da_ref[at, :] = da
        return (
            s_bo + fold_rows(da.astype(F32)),
            s_gain + fold_rows(dh * hat),
            s_shift + fold_rows(dh),
            s_bdown + fold_rows(dy),
        )

    carry = lax.fori_loop(0, rows // chunk, finish, (zero, zero, zero, zero))
    for n in range(4):
        sums_ref[8 * n:8 * n + 8, :] = carry[n]
    outs = [
        pltpu.make_async_copy(act_ref, act_out, sem_w.at[0]),
        pltpu.make_async_copy(dx1_ref, dx1_out, sem_w.at[1]),
        pltpu.make_async_copy(do_ref, do_out, sem_w.at[2]),
    ]
    outs[0].start()
    outs[1].start()
    for half in range(2):
        c = slice(half * width // 2, (half + 1) * width // 2)
        res = dot_nt(da_ref[...], wo[c, :]).astype(BF16)
        for d in range(nd // 2):
            do_ref[half * (nd // 2) + d] = res[:, d * lanes:(d + 1) * lanes]
    outs[2].start()
    left(0, full)
    left(1, full)
    half_rows = width // 2
    for half in range(2):
        res = dot_nn(attt[half * half_rows:(half + 1) * half_rows, :], da_ref[...]).astype(BF16)
        put(half, 0, res, per // 2, per)

        for i in range(per // 2):
            for j in range(per):
                leave(half, i * per + j, first_o + (half * (per // 2) + i) * per + j)
    for half in range(2):
        left(half, per * per // 2)
    for copy in outs:
        copy.wait()


def run_mlp(slot_of, att, x, dy, vec, gath, nd):
    rows, width = x.shape
    side = gath.shape[1]
    lanes = width // nd
    per = width // side
    first_o = 3 * per * per
    first_up = first_o + per * per
    first_dn = first_up + per * (FF // side)
    tile = width
    f32_rows = pltpu.VMEM((rows, width), F32)
    bf16_rows = pltpu.VMEM((rows, width), BF16)
    turned = pltpu.VMEM((width, rows), BF16)
    return pl.pallas_call(
        functools.partial(
            mlp_kernel, nd=nd, first_o=first_o, first_up=first_up, first_dn=first_dn, tile=tile
        ),
        out_shape=(
            sds((rows, width), BF16),
            sds((rows, width), F32),
            sds((nd, rows, lanes), BF16),
            sds((8 * (4 + FF // width), width), F32),
            sds(gath.shape, BF16),
        ),
        in_specs=[smem(), hbm(), hbm(), hbm(), vmem(), hbm()],
        out_specs=(hbm(), hbm(), hbm(), vmem(), hbm()),
        scratch_shapes=[
            bf16_rows,
            bf16_rows,
            bf16_rows,
            pltpu.SemaphoreType.DMA((3,)),
            pltpu.VMEM((width, width), BF16),
            pltpu.VMEM((3, width, tile), BF16),
            pltpu.VMEM((3, tile, width), BF16),
            f32_rows,
            f32_rows,
            f32_rows,
            bf16_rows,
            turned,
            turned,
            bf16_rows,
            pltpu.VMEM((rows, tile), F32),
            pltpu.VMEM((rows, tile), F32),
            pltpu.VMEM((2, rows, tile), BF16),
            pltpu.VMEM((2, rows, tile), BF16),
            pltpu.VMEM((nd, rows, lanes), BF16),
            pltpu.VMEM((2, 2 * per * (tile // side), side, side), BF16),
            pltpu.SemaphoreType.DMA((1,)),
            pltpu.SemaphoreType.DMA((FF // tile,)),
            pltpu.SemaphoreType.DMA((2,)),
            pltpu.SemaphoreType.DMA((3,)),
        ],
        compiler_params=params(),
        name="mlp",
    )(slot_of, att, x, dy, vec, gath)


def dh1_dot(cat, w, dh1, part, half):
    width = dh1.shape[1]
    c = slice(half * width // 2, (half + 1) * width // 2)
    res = dot_nt(cat[:, part * width:(part + 1) * width], w[part, c, :])
    if part == 0:
        dh1[:, c] = res
    else:
        dh1[:, c] += res


def first_norm_back(cat, x, dh1, dx1, ig, vec_ref):
    rows, width = x.shape
    chunk = 128
    zero = jnp.zeros((8, width), F32)

    def finish(r, carry):
        s_gain, s_shift, s_bq, s_bv = carry
        at = pl.ds(pl.multiple_of(r * chunk, chunk), chunk)
        centred, inv = layer_stats(x[at, :].astype(F32))
        hat = centred * inv
        dh = dh1[at, :]
        dhg = dh * vec_ref[GAIN1:GAIN1 + 1, :]
        back = inv * (
            dhg
            - jnp.mean(dhg, axis=-1, keepdims=True)
            - hat * jnp.mean(dhg * hat, axis=-1, keepdims=True)
        )
        ig[at, :] = dx1[at, :] + back
        return (
            s_gain + fold_rows(dh * hat),
            s_shift + fold_rows(dh),
            s_bq + fold_rows(cat[at, 0:width].astype(F32)),
            s_bv + fold_rows(cat[at, 2 * width:3 * width].astype(F32)),
        )

    return lax.fori_loop(0, rows // chunk, finish, (zero, zero, zero, zero))


def vector_rows(first, sums2):
    rows = [jnp.sum(v, axis=0, keepdims=True) for v in first]
    rows += [jnp.sum(sums2[8 * n:8 * n + 8, :], axis=0, keepdims=True) for n in range(sums2.shape[0] // 8)]
    return rows


def dh1_kernel(cat_ref, x_ref, dx1_ref, vec_ref, wq_ref, sums2_ref, ig_ref, vsum_ref, dh1):
    for part in range(3):
        for half in range(2):
            dh1_dot(cat_ref, wq_ref, dh1, part, half)
    first = first_norm_back(cat_ref, x_ref, dh1, dx1_ref, ig_ref, vec_ref)
    for n, row in enumerate(vector_rows(first, sums2_ref)):
        vsum_ref[n:n + 1, :] = row


def run_dh1(cat, x, dx1, vec, wq, sums2):
    rows, width = x.shape
    return pl.pallas_call(
        dh1_kernel,
        out_shape=(sds((rows, width), F32), sds(vec.shape, F32)),
        in_specs=[vmem()] * 6,
        out_specs=(vmem(), vmem()),
        scratch_shapes=[pltpu.VMEM((rows, width), F32)],
        compiler_params=params(),
        name="dh1",
    )(cat, x, dx1, vec, wq, sums2)


def wgrad_kernel(slot_ref, h1_ref, cat_ref, rest, out, a_t, stage, sem_out, *, side, tile):
    del rest
    rows, width = h1_ref.shape
    per = width // side
    cols = tile // side
    steps = cat_ref.shape[1] // tile
    for r in range(width // 256):
        c = slice(r * 256, (r + 1) * 256)
        a_t[c, :] = turn(h1_ref[:, c])

    def left(slot):
        pltpu.make_async_copy(stage.at[slot], stage.at[slot], sem_out.at[slot]).wait()

    @pl.loop(0, steps)
    def _(t):
        slot = lax.rem(t, 2)

        @pl.when(t >= 2)
        def _():
            left(slot)
        res = dot_nn(a_t[...], cat_ref[:, pl.ds(pl.multiple_of(t * tile, tile), tile)]).astype(BF16)
        for i in range(per):
            for j in range(cols):
                stage[slot, i * cols + j] = res[i * side:(i + 1) * side, j * side:(j + 1) * side]

        for i in range(per):
            for j in range(cols):
                dst = slot_at(slot_ref, i * 3 * per + t * cols + j)
                pltpu.make_async_copy(stage.at[slot, i * cols + j], out.at[dst], sem_out.at[slot]).start()

    left(0)
    left(1)


def run_wgrad(slot_of, h1, cat, grads):
    rows, width = h1.shape
    side = grads.shape[1]
    tile = 512
    return pl.pallas_call(
        functools.partial(wgrad_kernel, side=side, tile=tile),
        out_shape=sds(grads.shape, BF16),
        in_specs=[smem(), vmem(), vmem(), hbm()],
        out_specs=hbm(),
        scratch_shapes=[
            pltpu.VMEM((width, rows), BF16),
            pltpu.VMEM((2, (width // side) * (tile // side), side, side), BF16),
            pltpu.SemaphoreType.DMA((2,)),
        ],
        input_output_aliases={3: 0},
        compiler_params=params(),
        name="wgrad",
    )(slot_of, h1, cat, grads)


def whereami():
    g = lax.axis_index("grp")
    d = lax.axis_index("dev")
    core = lax.rem(d, 2)
    x = lax.rem(d // 2, 2)
    y = d // 4
    over_x = d + 2 - 4 * x
    over_y = d + 4 - 8 * y
    across = over_x + 4 - 8 * y
    sibling = d + 1 - 2 * core
    return g, d, over_x, over_y, across, sibling


def near_order(t, g, ng):
    t = ng - 1 - t
    low = jnp.where(t < ng - 1 - g, ng - 1 - t, t - (ng - 1 - g))
    high = jnp.where(t < g, t, ng - 1 - (t - g))
    return jnp.where(2 * g < ng, low, high)


def greet(g, ng, peers):
    barrier = pltpu.get_barrier_semaphore()
    for peer in peers:
        pl.semaphore_signal(barrier, inc=1, device_id=(g, peer), device_id_type=MESH)

    d = lax.axis_index("dev")

    @pl.when(g > 0)
    def _():
        pl.semaphore_signal(barrier, inc=1, device_id=(g - 1, d), device_id_type=MESH)

    @pl.when(g < ng - 1)
    def _():
        pl.semaphore_signal(barrier, inc=1, device_id=(g + 1, d), device_id_type=MESH)

    ends = (g > 0).astype(jnp.int32) + (g < ng - 1).astype(jnp.int32)
    pl.semaphore_wait(barrier, len(peers) + ends)


def slot_cuts(count):
    third = 2 * (count // 12)
    first = (count - third) // 2
    return first, count - third - first, third // 2, third // 2


def gather_kernel(
    w_ref, x_ref, block_ref, vin_ref, out, h1_ref, slot_ref, vec_ref,
    own, local_sem, zs, zr, cs, cr, ss, sr, *, ng, nd
):
    count = w_ref.shape[0]
    na, nb, nc1, nc2 = slot_cuts(count)
    flat = na + nb
    nc = nc1 + nc2
    g, d, over_x, over_y, across, sibling = whereami()
    columns = (d, over_x, over_y, across)
    own[...] = w_ref[...].astype(BF16)
    greet(g, ng, (over_x, over_y, sibling))

    def region(gz, dev, first=0, size=count):
        return out.at[pl.ds((gz * nd + dev) * count + first, size)]

    def wide(t):
        return count if t == 0 else flat

    def kind(n, t):
        return (
            (d, 0, wide(t), over_x),
            (d, 0, wide(t), over_y),
            (d, 0, wide(t), sibling),
            (over_x, 0, na, over_y),
            (over_y, na, nb, over_x),
            (over_x, 0, wide(t), sibling),
            (over_y, 0, wide(t), sibling),
            (across, 0, na, sibling),
            (across, na, nb, sibling),
            (over_x, flat, nc1, over_y),
            (over_y, flat + nc1, nc2, over_x),
            (across, flat, nc1, sibling),
            (across, flat + nc1, nc2, sibling),
            (d, flat, nc, sibling),
            (over_x, flat, nc, sibling),
            (over_y, flat, nc, sibling),
            (across, flat, nc, sibling),
        )[n]

    def kinds(t):
        return range(13) if t == 0 else tuple(range(9)) + tuple(range(13, 17))

    def plane(n, t, src=None):
        gz = near_order(t, g, ng)
        dev, first, size, to = kind(n, t)
        at = region(gz, dev, first, size)
        return remote(at if src is None else src, at, ss.at[n, gz], sr.at[n, gz], (g, to))

    def landed(n, t, dev):
        gz = near_order(t, g, ng)
        _, first, size, _ = kind(n, t)
        arrived(region(gz, dev, first, size), sr.at[n, gz])

    def line(gz, up, src=None):
        at = region(gz, d, 0, flat)
        to = g + 1 if up else g - 1
        return remote(at if src is None else src, at, zs.at[gz, int(up)], zr.at[gz], (to, d))

    def corner_line(gz, c, up, src=None):
        at = region(gz, columns[c], flat, nc)
        to = g + 1 if up else g - 1
        return remote(at if src is None else src, at, cs.at[gz, c, int(up)], cr.at[gz, c], (to, d))

    def both_ways(gz, make):
        @pl.when((gz <= g) & (g < ng - 1))
        def _():
            make(True)

        @pl.when((gz >= g) & (g > 0))
        def _():
            make(False)

    mine = pltpu.make_async_copy(own, region(g, d), local_sem.at[0])
    mine.start()

    def column(t):
        gz = near_order(t, g, ng)
        if t == 0:
            both_ways(gz, lambda up: line(gz, up, cut(own, 0, flat)).start())
            for n in range(3):
                plane(n, t, own).start()
            both_ways(gz, lambda up: corner_line(gz, 0, up, cut(own, flat, nc)).start())
            return
        arrived(region(gz, d, 0, flat), zr.at[gz])
        both_ways(gz, lambda up: line(gz, up).start())
        for n in range(3):
            plane(n, t).start()

    def sides(t):
        gz = near_order(t, g, ng)
        landed(0, t, over_x)
        plane(3, t).start()
        if t == 0:
            plane(9, t).start()
            both_ways(gz, lambda up: corner_line(gz, 1, up).start())
        plane(5, t).start()
        landed(1, t, over_y)
        plane(4, t).start()
        if t == 0:
            plane(10, t).start()
            both_ways(gz, lambda up: corner_line(gz, 2, up).start())
        plane(6, t).start()

    def corner(t):
        gz = near_order(t, g, ng)
        if t == 0:
            landed(9, t, across)
            landed(10, t, across)
            both_ways(gz, lambda up: corner_line(gz, 3, up).start())
            plane(11, t).start()
            plane(12, t).start()
        landed(3, t, across)
        plane(7, t).start()
        landed(4, t, across)
        plane(8, t).start()

    def far_corner(t):
        gz = near_order(t, g, ng)
        for c in range(4):
            arrived(region(gz, columns[c], flat, nc), cr.at[gz, c])
            both_ways(gz, lambda up: corner_line(gz, c, up).start())
            plane(13 + c, t).start()

    plan = [(t, f) for t in range(ng) for f in (0, 1, 2, 3) if t > 0 or f < 3]
    lag = {0: 0, 1: 1.5, 2: 2.6, 3: 2.2}
    for t, f in sorted(plan, key=lambda e: e[0] * 1.0 + lag[e[1]]):
        (column, sides, corner, far_corner)[f](t)
        if (t, f) == (0, 0):
            prepare(x_ref, block_ref, vin_ref, h1_ref, slot_ref, vec_ref)

    for t in range(ng):
        for n in kinds(t):
            dev, _, _, to = kind(n, t)
            if to is sibling:
                landed(n, t, dev + sibling - d)
    mine.wait()
    for t in range(ng):
        gz = near_order(t, g, ng)
        for n in kinds(t):
            plane(n, t).wait_send()
        both_ways(gz, lambda up: line(gz, up).wait_send())
        for c in range(4):
            both_ways(gz, lambda up: corner_line(gz, c, up).wait_send())


def run_gather(w, x, blocks, vin, ng, nd):
    count, side, _ = w.shape
    dma = pltpu.SemaphoreType.DMA
    return pl.pallas_call(
        functools.partial(gather_kernel, ng=ng, nd=nd),
        out_shape=(sds((ng * nd * count, side, side), BF16),) + prepared_shapes(x, blocks, vin),
        in_specs=[vmem()] * 4,
        out_specs=(hbm(), vmem(), vmem(), vmem()),
        scratch_shapes=[
            pltpu.VMEM((count, side, side), BF16),
            dma((1,)),
            dma((ng, 2)),
            dma((ng,)),
            dma((ng, 4, 2)),
            dma((ng, 4)),
            dma((17, ng)),
            dma((17, ng)),
        ],
        compiler_params=params(collective_id=0, has_side_effects=True),
        name="gather",
    )(w, x, blocks, vin)


def add_blocks(dst, src, size):
    step = next(n for n in (4, 5, 3, 2, 1) if size % n == 0)

    @pl.loop(0, size // step)
    def _(n):
        for k in range(step):
            dst[n * step + k] = dst[n * step + k] + src[n * step + k]


def scatter_kernel(
    grads, sums2_ref, vec_ref, vin_ref, cat_in, x_in, dx1_in, wq_in, out_ref, vout_ref, vnew_ref, ig_out,
    cat, x, dx1, wq, dh1, sem_in, mine, r0, r1y, r1x, r2x, r2y, rz, cz, cy, cx, cx2, cy2, vwork, vxy, vz,
    load, s0, w0, s1, w1, s2, w2, sz, wz, sc, wc, s3, w3, vs, vw, *, ng, nd, rate
):
    count = out_ref.shape[0]
    na, nb, nc1, nc2 = slot_cuts(count)
    flat = na + nb
    nc = nc1 + nc2
    g, d, over_x, over_y, across, sibling = whereami()
    columns = (d, over_x, over_y, across)

    def region(gz, dev):
        return grads.at[pl.ds((gz * nd + dev) * count, count)]

    def order(t):
        return near_order(ng - 1 - t, g, ng)

    for t in range(ng):
        for c in range(4):
            pltpu.make_async_copy(region(order(t), columns[c]), mine.at[order(t), c], load.at[order(t), c]).start()
    greet(g, ng, (over_x, over_y, sibling))

    def to_sibling(gz, c):
        return remote(
            region(gz, columns[c] + sibling - d), r0.at[gz, c], s0.at[gz, c], w0.at[gz, c], (g, sibling)
        )

    peers = (sibling, over_x, over_y)

    def vec_copy(n):
        return remote(vwork.at[n], vxy.at[n], vs.at[n], vw.at[n], (g, peers[n]))

    for t in range(ng):
        for c in (3, 2, 1, 0):
            to_sibling(order(t), c).start()
    inputs = [
        pltpu.make_async_copy(cat_in, cat, sem_in.at[0]),
        pltpu.make_async_copy(wq_in, wq, sem_in.at[1]),
        pltpu.make_async_copy(x_in, x, sem_in.at[2]),
        pltpu.make_async_copy(dx1_in, dx1, sem_in.at[3]),
    ]
    for copy in inputs:
        copy.start()
    input_grad = pltpu.make_async_copy(dx1, ig_out, sem_in.at[4])

    def first_norm():
        for copy in inputs:
            copy.wait()
        for part in range(3):
            for half in range(2):
                dh1_dot(cat, wq, dh1, part, half)
        first = first_norm_back(cat, x, dh1, dx1, dx1, vec_ref)
        input_grad.start()
        for n, row in enumerate(vector_rows(first, sums2_ref)):
            vwork[0, n:n + 1, :] = row
        vec_copy(0).start()

    first = (
        (2, 0, na, r1y, 0, over_y),
        (3, 0, na, r1y, 1, over_y),
        (1, na, nb, r1x, 0, over_x),
        (3, na, nb, r1x, 1, over_x),
    )
    second = ((1, 0, na, r2x, over_x), (2, na, nb, r2y, over_y))
    third = (
        (2, flat, nc1, cy.at[0], over_y),
        (3, flat, nc1, cy.at[1], over_y),
        (1, flat + nc1, nc2, cx.at[0], over_x),
        (3, flat + nc1, nc2, cx.at[1], over_x),
        (1, flat, nc1, cx2, over_x),
        (2, flat + nc1, nc2, cy2, over_y),
    )

    def copy1(n, gz):
        c, at, size, buf, place_at, to = first[n]
        return remote(cut(mine.at[gz, c], at, size), buf.at[gz, place_at], s1.at[n, gz], w1.at[n, gz], (g, to))

    def copy2(n, gz):
        c, at, size, buf, to = second[n]
        return remote(cut(mine.at[gz, c], at, size), buf.at[gz], s2.at[n, gz], w2.at[n, gz], (g, to))

    def copy3(n):
        c, at, size, buf, to = third[n]
        return remote(cut(mine.at[g, c], at, size), buf, s3.at[n], w3.at[n], (g, to))

    def flat_part(gz):
        return cut(mine.at[gz, 0], 0, flat)

    def corner_part(gz):
        return mine.at[gz, :, pl.ds(flat, nc)]

    def line(gz, part, buf, sends, waits, up):
        at = gz if up else jnp.where(gz < g - 1, gz, ng)
        to = g + 1 if up else g - 1
        return remote(part(gz), buf.at[at], sends.at[gz], waits.at[at], (to, d))

    def pass_on(gz, part, buf, sends, waits, gather):
        @pl.when(gz > g)
        def _():
            @pl.when(g > 0)
            def _():
                arrived(buf.at[gz], waits.at[gz])
                gather(gz)
            line(gz, part, buf, sends, waits, True).start()

        @pl.when(gz < g)
        def _():
            @pl.when(g < ng - 1)
            def _():
                arrived(buf.at[gz], waits.at[gz])
                gather(gz)
            line(gz, part, buf, sends, waits, False).start()

    def gather_flat(gz):
        add_blocks(flat_part(gz), rz.at[gz], flat)

    def gather_corner(at, gz):
        for c in range(4):
            add_blocks(cut(mine.at[gz, c], flat, nc), cz.at[at, c], nc)

    def sums0(t, c):
        gz = order(t)
        pltpu.make_async_copy(region(gz, columns[c]), mine.at[gz, c], load.at[gz, c]).wait()
        arrived(r0.at[gz, c], w0.at[gz, c])
        add_blocks(mine.at[gz, c], r0.at[gz, c], count)
        for n in {3: (1, 3), 2: (0,), 1: (2,), 0: ()}[c]:
            copy1(n, gz).start()

    def along0(t):
        pass_on(order(t), corner_part, cz, sc, wc, lambda gz: gather_corner(gz, gz))

    def stage1(t, k):
        gz = order(t)
        c, at, size, buf, n = (
            (1, 0, na, r1y.at[gz, 1], 1),
            (2, na, nb, r1x.at[gz, 1], 3),
            (0, 0, na, r1y.at[gz, 0], 0),
            (0, na, nb, r1x.at[gz, 0], 2),
        )[k]
        arrived(buf, w1.at[n, gz])
        add_blocks(cut(mine.at[gz, c], at, size), buf, size)
        if k < 2:
            copy2(k, gz).start()

    def stage2(t, k):
        gz = order(t)
        at, size, buf = ((0, na, r2x.at[gz]), (na, nb, r2y.at[gz]))[k]
        arrived(buf, w2.at[k, gz])
        add_blocks(cut(mine.at[gz, 0], at, size), buf, size)

    def along1(t):
        pass_on(order(t), flat_part, rz, sz, wz, gather_flat)

    def corner0():
        @pl.when(g > 0)
        def _():
            arrived(cz.at[g], wc.at[g])
            gather_corner(g, g)

        @pl.when(g < ng - 1)
        def _():
            arrived(cz.at[ng], wc.at[ng])
            gather_corner(ng, g)
        for n in range(4):
            copy3(n).start()

    def corner1():
        arrived(cy.at[1], w3.at[1])
        add_blocks(cut(mine.at[g, 1], flat, nc1), cy.at[1], nc1)
        copy3(4).start()
        arrived(cx.at[1], w3.at[3])
        add_blocks(cut(mine.at[g, 2], flat + nc1, nc2), cx.at[1], nc2)
        copy3(5).start()
        arrived(cy.at[0], w3.at[0])
        add_blocks(cut(mine.at[g, 0], flat, nc1), cy.at[0], nc1)
        arrived(cx.at[0], w3.at[2])
        add_blocks(cut(mine.at[g, 0], flat + nc1, nc2), cx.at[0], nc2)

    def corner2():
        arrived(cx2, w3.at[4])
        add_blocks(cut(mine.at[g, 0], flat, nc1), cx2, nc1)
        arrived(cy2, w3.at[5])
        add_blocks(cut(mine.at[g, 0], flat + nc1, nc2), cy2, nc2)

    def vec_step(n):
        arrived(vxy.at[n], vw.at[n])
        total = vwork[n] + vxy[n]
        if n < 2:
            vwork[n + 1] = total
            vec_copy(n + 1).start()
        else:
            vz[g] = total

    def vec_line(gz, up):
        to = g + 1 if up else g - 1
        return remote(vz.at[gz], vz.at[gz], vs.at[3 + 2 * gz + int(up)], vw.at[3 + gz], (to, d))

    def vec_first_line():
        vec_step(2)

        @pl.when(g < ng - 1)
        def _():
            vec_line(g, True).start()

        @pl.when(g > 0)
        def _():
            vec_line(g, False).start()

    def vec_next_line(n):
        gz = near_order(n, g, ng)
        arrived(vz.at[gz], vw.at[3 + gz])

        @pl.when((gz < g) & (g < ng - 1))
        def _():
            vec_line(gz, True).start()

        @pl.when((gz > g) & (g > 0))
        def _():
            vec_line(gz, False).start()

    def vec_out():
        total = vz[0]
        for z in range(1, ng):
            total = total + vz[z]
        vwork[3] = total
        per = total.shape[1] // 128
        for r in range(total.shape[0]):
            for c in range(per):
                row = vwork[3, r:r + 1, c * 128:(c + 1) * 128]
                n = per * r + c
                vout_ref[n:n + 1, :] = row
                vnew_ref[n:n + 1, :] = vin_ref[n:n + 1, :] - rate * row

    last = ng - 1
    plan = [(t + 0.25 * (3 - c), sums0, (t, c)) for t in range(ng) for c in range(4)]
    plan += [(t + 1.2 + 0.3 * (k // 2), stage1, (t, k)) for t in range(ng) for k in range(4)]
    plan += [(t + 2.2, stage2, (t, k)) for t in range(ng) for k in range(2)]
    plan += [(t + 1.15, along0, (t,)) for t in range(last)]
    plan += [(t + 2.21, along1, (t,)) for t in range(last)]
    plan += [(last + 1.3, corner0, ()), (last + 2.19, corner1, ()), (last + 2.4, corner2, ())]
    plan += [(0.3, first_norm, ()), (0.9, vec_step, (0,)), (2.0, vec_step, (1,)), (3.0, vec_first_line, ())]
    plan += [(3.1 + 0.55 * n, vec_next_line, (n,)) for n in range(1, ng)]
    plan += [(last + 2.17, vec_out, ())]
    plan = [(step, args) for _, step, args in sorted(plan, key=lambda e: e[0])]
    if ng == 4:
        plan = [
            (sums0, (0, 3)), (sums0, (0, 2)), (first_norm, ()), (sums0, (0, 1)),
            (sums0, (0, 0)), (stage1, (0, 1)), (sums0, (1, 3)), (vec_step, (0,)),
            (along0, (0,)), (stage1, (0, 0)), (sums0, (1, 2)), (sums0, (1, 0)),
            (sums0, (1, 1)), (along0, (1,)), (stage1, (1, 1)), (stage1, (0, 3)),
            (vec_step, (1,)), (sums0, (2, 3)), (stage2, (0, 0)), (stage1, (1, 0)),
            (stage1, (0, 2)), (stage2, (0, 1)), (sums0, (2, 1)), (along1, (0,)),
            (sums0, (2, 2)), (sums0, (2, 0)), (along0, (2,)), (stage1, (1, 2)), (vec_first_line, ()),
            (sums0, (3, 3)), (stage2, (1, 0)), (sums0, (3, 0)),
            (stage1, (2, 1)), (sums0, (3, 2)), (stage1, (2, 0)),
            (stage1, (1, 3)), (stage2, (1, 1)), (stage1, (2, 2)), (vec_next_line, (1,)), (sums0, (3, 1)),
            (along1, (1,)), (stage2, (2, 0)), (stage2, (2, 1)), (stage1, (2, 3)),
            (stage1, (3, 1)), (along1, (2,)), (corner0, ()), (vec_next_line, (2,)),
            (stage1, (3, 0)), (stage2, (3, 1)), (stage1, (3, 2)), (stage1, (3, 3)),
            (vec_next_line, (3,)), (corner1, ()), (vec_out, ()), (corner2, ()),
            (stage2, (3, 0)),
        ]
    for step, args in plan:
        step(*args)

    @pl.when(g > 0)
    def _():
        arrived(rz.at[g], wz.at[g])

    @pl.when(g < ng - 1)
    def _():
        arrived(rz.at[ng], wz.at[ng])

    @pl.when((g > 0) & (g < ng - 1))
    def _():
        @pl.loop(0, flat)
        def _(i):
            out_ref[i] = mine[g, 0, i].astype(F32) + rz[g, i].astype(F32) + rz[ng, i].astype(F32)

    @pl.when(g == 0)
    def _():
        @pl.loop(0, flat)
        def _(i):
            out_ref[i] = mine[g, 0, i].astype(F32) + rz[ng, i].astype(F32)

    @pl.when((g > 0) & (g == ng - 1))
    def _():
        @pl.loop(0, flat)
        def _(i):
            out_ref[i] = mine[g, 0, i].astype(F32) + rz[g, i].astype(F32)

    for i in range(flat, count):
        out_ref[i] = mine[g, 0, i].astype(F32)

    for t in range(ng):
        gz = order(t)
        for c in range(4):
            to_sibling(gz, c).wait_send()
        for n in range(4):
            copy1(n, gz).wait_send()
        for n in range(2):
            copy2(n, gz).wait_send()
        if t < ng - 1:
            arrived(flat_part(gz), sz.at[gz])
            arrived(corner_part(gz), sc.at[gz])
    input_grad.wait()
    for n in range(6):
        copy3(n).wait_send()
    for n in range(3):
        vec_copy(n).wait_send()
    for n in range(ng):
        gz = near_order(n, g, ng)

        @pl.when((gz <= g) & (g < ng - 1))
        def _():
            vec_line(gz, True).wait_send()

        @pl.when((gz >= g) & (g > 0))
        def _():
            vec_line(gz, False).wait_send()


def run_scatter(grads, sums2, vec, vin, cat, x, dx1, wq, ng, nd, rate):
    blocks, side, _ = grads.shape
    count = blocks // (ng * nd)
    na, nb, nc1, nc2 = slot_cuts(count)
    flat = na + nb
    dma = pltpu.SemaphoreType.DMA

    def buf(*lead):
        return pltpu.VMEM(lead + (side, side), BF16)

    def like(v):
        return pltpu.VMEM(v.shape, v.dtype)

    return pl.pallas_call(
        functools.partial(scatter_kernel, ng=ng, nd=nd, rate=rate),
        out_shape=(
            sds((count, side, side), F32),
            sds(vin.shape, F32),
            sds(vin.shape, F32),
            sds(dx1.shape, F32),
        ),
        in_specs=[hbm(), vmem(), vmem(), vmem()] + [hbm()] * 4,
        out_specs=(vmem(), vmem(), vmem(), hbm()),
        scratch_shapes=[
            like(cat),
            like(x),
            like(dx1),
            like(wq),
            like(dx1),
            dma((5,)),
            buf(ng, 4, count),
            buf(ng, 4, count),
            buf(ng, 2, na),
            buf(ng, 2, nb),
            buf(ng, na),
            buf(ng, nb),
            buf(ng + 1, flat),
            buf(ng + 1, 4, nc1 + nc2),
            buf(2, nc1),
            buf(2, nc2),
            buf(nc1),
            buf(nc2),
            pltpu.VMEM((4,) + vec.shape, F32),
            pltpu.VMEM((3,) + vec.shape, F32),
            pltpu.VMEM((ng,) + vec.shape, F32),
            dma((ng, 4)),
            dma((ng, 4)),
            dma((ng, 4)),
            dma((4, ng)),
            dma((4, ng)),
            dma((2, ng)),
            dma((2, ng)),
            dma((ng,)),
            dma((ng + 1,)),
            dma((ng,)),
            dma((ng + 1,)),
            dma((6,)),
            dma((6,)),
            dma((3 + 2 * ng,)),
            dma((3 + ng,)),
        ],
        compiler_params=params(61, collective_id=1, has_side_effects=True),
        name="scatter",
    )(grads, sums2, vec, vin, cat, x, dx1, wq)


def blocks_kernel(*refs, handed):
    g_ref, w_ref, ls_ref, rs_ref, lr_ref, rr_ref = refs[:6]
    wg_out, nl_out, nr_out, nw_out = refs[6 + handed:10 + handed]
    for n in range(handed):
        refs[10 + handed + n][...] = refs[6 + n][...]

    for i in range(g_ref.shape[0]):
        grad = g_ref[i]
        wg_out[i] = grad
        hi = grad.astype(BF16)
        low = (grad - hi.astype(F32)).astype(BF16)
        nl_out[i] = 0.5 * ls_ref[i] + 0.5 * dot_nt(hi, hi)
        turned = grad.T
        hi_t = turned.astype(BF16)
        nr_out[i] = 0.5 * rs_ref[i] + 0.5 * dot_nt(hi_t, hi_t)
        left = lr_ref[i]
        left_hi = left.astype(BF16)
        left_low = (left - left_hi.astype(F32)).astype(BF16)
        shaped = dot_nn(left_hi, hi) + dot_nn(left_hi, low) + dot_nn(left_low, hi)
        right = rr_ref[i]
        right_hi = right.astype(BF16)
        right_low = (right - right_hi.astype(F32)).astype(BF16)
        sh_hi = shaped.astype(BF16)
        sh_low = (shaped - sh_hi.astype(F32)).astype(BF16)
        shaped = dot_nn(sh_hi, right_hi) + dot_nn(sh_low, right_hi) + dot_nn(sh_hi, right_low)
        nw_out[i] = w_ref[i] - weight_rate * shaped


def run_blocks(grads, weights, left_stats, right_stats, left_roots, right_roots, *passing):
    count, side, _ = grads.shape
    steps = math.gcd(count, 4)
    step = count // steps
    spec = pl.BlockSpec((step, side, side), lambda n: (n, 0, 0))
    through = []
    for v in passing:
        part = v.shape[0] // steps
        if part % 8 == 0:
            through.append(pl.BlockSpec((part, v.shape[1]), lambda n: (n, 0)))
        else:
            through.append(pl.BlockSpec(v.shape, lambda n: (0, 0)))
    return pl.pallas_call(
        functools.partial(blocks_kernel, handed=len(passing)),
        grid=(steps,),
        out_shape=tuple([sds(grads.shape, F32)] * 4) + tuple(sds(v.shape, v.dtype) for v in passing),
        in_specs=[spec] * 6 + through,
        out_specs=tuple([spec] * 4) + tuple(through),
        compiler_params=params(),
        name="blocks",
    )(grads, weights, left_stats, right_stats, left_roots, right_roots, *passing)


def local(
    inputs,
    cotangent,
    weight_slots,
    slot_block,
    left_stats,
    right_stats,
    left_roots,
    right_roots,
    vectors,
    span_start,
):
    seq_count, tok_count, width = inputs.shape
    rows = seq_count * tok_count
    nd = lax.axis_size("dev")
    ng = lax.axis_size("grp")
    side = weight_slots.shape[1]
    hpd = H // nd
    lanes = width // nd
    head = lax.axis_index("dev") * hpd + jnp.arange(hpd, dtype=jnp.int32)
    slopes = jnp.exp2(-8.0 * (head.astype(F32) + 1.0) / H)
    vin = vectors.reshape(-1, 128)
    held = slot_block.reshape(-1, 128)
    x = inputs.reshape(rows, width)
    dy = cotangent.reshape(rows, width)
    rate = vector_rate / math.sqrt(rows * nd * ng)

    direct = nd == 8
    if direct:
        gath, h1, slot_of, vec = run_gather(weight_slots, x, held, vin, ng, nd)
    else:
        gath = lax.all_gather(weight_slots.astype(BF16), ("grp", "dev"), axis=0, tiled=True)
        h1, slot_of, vec = run_prepare(x, held, vin)
    qkv, wq = run_qkv(slot_of, h1, vec, gath, nd)
    qkv, o, o32, lse = run_attn_fwd(
        span_start, slopes, qkv.reshape(nd, 3, seq_count, tok_count, lanes), hpd
    )
    att = side_by_side(o, 1, rows)
    act, dx1, do, sums2, grads = run_mlp(slot_of, att, x, dy, vec, gath, nd)
    do = do.reshape(nd, seq_count, tok_count, lanes)
    cat = side_by_side(run_attn_bwd(span_start, slopes, qkv, do, o32, lse, hpd), 3, rows)
    grads = run_wgrad(slot_of, h1, cat, grads)
    if direct:
        weight_grads, vector_grads, new_vectors, ig = run_scatter(
            grads, sums2, vec, vin, cat, x, dx1, wq, ng, nd, rate
        )
        passing = (ig, vector_grads, new_vectors)
    else:
        ig, vsum = run_dh1(cat, x, dx1, vec, wq, sums2)
        vector_grads = lax.psum(vsum.reshape(-1), ("grp", "dev"))
        new_vectors = vectors - rate * vector_grads
        weight_grads = lax.psum_scatter(grads, ("grp", "dev"), scatter_dimension=0, tiled=True)
        weight_grads = weight_grads.astype(F32)
        passing = ()
    weight_grads, new_left, new_right, new_weights, *passed = run_blocks(
        weight_grads, weight_slots, left_stats, right_stats, left_roots, right_roots, *passing
    )
    if direct:
        ig, vector_grads, new_vectors = passed
    return (
        act.reshape(inputs.shape),
        ig.reshape(inputs.shape),
        weight_grads,
        new_left,
        new_right,
        new_weights,
        vector_grads.reshape(-1),
        new_vectors.reshape(-1),
    )


def solution(mesh):
    return jax.shard_map(
        local,
        mesh=mesh,
        in_specs=(
            P("grp", "dev", None),
            P("grp", "dev", None),
            P(("grp", "dev"), None, None),
            P(),
            P(("grp", "dev"), None, None),
            P(("grp", "dev"), None, None),
            P(("grp", "dev"), None, None),
            P(("grp", "dev"), None, None),
            P(),
            P("grp"),
        ),
        out_specs=(
            P("grp", "dev", None),
            P("grp", "dev", None),
            P(("grp", "dev"), None, None),
            P(("grp", "dev"), None, None),
            P(("grp", "dev"), None, None),
            P(("grp", "dev"), None, None),
            P(),
            P(),
        ),
        check_vma=False,
    )
```

profile of v0, /device:TPU:0, one launch (start us, length us, event | category | flops | bytes accessed | tf_op | source)
XLA Modules:
  0.0 414.4 jit_solution(6769251782706497836)
XLA Ops:
  0.6 0.5 multiply_exponential_fusion.slope_ref
  1.2 106.3 %gather.1 = (bf16[768,128,128]{2,1,0:T(8,128)(2,1)}, bf16[512,1024]{1,0:T(8,128)(2,1)}, s32[6,128]{1,0:T(8,128)}, f32[12,1024]{1,0:T(8,128)}) custom-call(f32[24,128,128]{2,1,0:T(8,128)} %refs_1_.1, bf16[512,1024]{1,0:T(8,128)(2,1)} %bitcast.10, s32[6,128]{1,0:T(8,128)} %bitcast.18, f32[96,128]{1,0:T(8,128)} %bitcast.16), custom_call_target="tpu_custom_call" | custom-call | tf_op jit(solution)/shard_map/gather/pallas_call | solution.py:1359
  107.5 8.3 %qkv.1 = (bf16[8,3,512,128]{3,2,1,0:T(8,128)(2,1)}, bf16[3,1024,1024]{2,1,0:T(8,128)(2,1)}) custom-call(s32[6,128]{1,0:T(8,128)} %get-tuple-element.34.slot_ref, bf16[512,1024]{1,0:T(8,128)(2,1)} %get-tuple-element.35.h1_ref, f32[12,1024]{1,0:T(8,128)} %get-tuple-element.36.vec_ref, bf16[768,128,128]{2,1,0:T(8,128)(2,1)} %get-tuple-element.37.gath), custom_call_target="tpu_custom_call" | custom-call | tf_op jit(solution)/shard_map/qkv/pallas_call | solution.py:166
  115.8 50.6 %attn_fwd.1 = (bf16[8,3,2,256,128]{4,3,2,1,0:T(8,128)(2,1)}, bf16[512,1024]{1,0:T(8,128)(2,1)}, f32[8,2,256,128]{3,2,1,0:T(8,128)}, f32[8,2,256,128]{3,2,1,0:T(8,128)}) custom-call(s32[2]{0:T(128)} %span_ref.3, f32[2]{0:T(128)} %multiply_exponential_fusion.slope_ref, bf16[8,3,2,256,128]{4,3,2,1,0:T(8,128)(2,1)} %bitcast.13), custom_call_target="tpu_custom_call" | custom-call | tf_op jit(solution)/shard_map/attn_fwd/pallas_call | solution.py:490
  166.4 48.7 %mlp.1 = (bf16[512,1024]{1,0:T(8,128)(2,1)}, f32[512,1024]{1,0:T(8,128)}, bf16[8,512,128]{2,1,0:T(8,128)(2,1)}, f32[64,1024]{1,0:T(8,128)}, bf16[768,128,128]{2,1,0:T(8,128)(2,1)}) custom-call(s32[6,128]{1,0:T(8,128)} %get-tuple-element.34.slot_ref, bf16[512,1024]{1,0:T(8,128)(2,1)} %get-tuple-element.39.att_in, bf16[512,1024]{1,0:T(8,128)(2,1)} %bitcast.11, ...), custom_call_target="tpu_custom_call" | custom-call | tf_op jit(solution)/shard_map/mlp/pallas_call | solution.py:1001
  215.1 65.7 %attn_bwd.1.cat_ref.cat_in = bf16[512,3072]{1,0:T(8,128)(2,1)} custom-call(s32[2]{0:T(128)} %span_ref.3, f32[2]{0:T(128)} %multiply_exponential_fusion.slope_ref, bf16[8,3,2,256,128]{4,3,2,1,0:T(8,128)(2,1)} %get-tuple-element.41.qkv_in, bf16[8,2,256,128]{3,2,1,0:T(8,128)(2,1)} %bitcast.14, f32[8,2,256,128]{3,2,1,0:T(8,128)} %get-tuple-element.43.o32_in, ...), custom_call_target="tpu_custom_call" | custom-call | tf_op jit(solution)/shard_map/attn_bwd/pallas_call | solution.py:727
  280.8 8.6 %wgrad.1.grads = bf16[768,128,128]{2,1,0:T(8,128)(2,1)} custom-call(s32[6,128]{1,0:T(8,128)} %get-tuple-element.34.slot_ref, bf16[512,1024]{1,0:T(8,128)(2,1)} %get-tuple-element.35.h1_ref, bf16[512,3072]{1,0:T(8,128)(2,1)} %attn_bwd.1.cat_ref.cat_in, bf16[768,128,128]{2,1,0:T(8,128)(2,1)} %get-tuple-element.45.rest), custom_call_target="tpu_custom_call", output_to_operand_aliasing={{}: (3, {})} | custom-call | tf_op jit(solution)/shard_map/wgrad/pallas_call | solution.py:1149
  289.4 116.1 %scatter.1 = (f32[24,128,128]{2,1,0:T(8,128)}, f32[96,128]{1,0:T(8,128)}, f32[96,128]{1,0:T(8,128)}, f32[512,1024]{1,0:T(8,128)}) custom-call(bf16[768,128,128]{2,1,0:T(8,128)(2,1)} %wgrad.1.grads, f32[64,1024]{1,0:T(8,128)} %get-tuple-element.46.sums2_ref, f32[12,1024]{1,0:T(8,128)} %get-tuple-element.36.vec_ref, f32[96,128]{1,0:T(8,128)} %bitcast.17, ...), custom_call_target="tpu_custom_call" | custom-call | tf_op jit(solution)/shard_map/scatter/pallas_call | solution.py:1724
  405.5 8.6 %blocks.1 = (f32[24,128,128]{2,1,0:T(8,128)}, f32[24,128,128]{2,1,0:T(8,128)}, f32[24,128,128]{2,1,0:T(8,128)}, f32[24,128,128]{2,1,0:T(8,128)}, f32[512,1024]{1...) custom-call(f32[24,128,128]{2,1,0:T(8,128)} %get-tuple-element.49.refs_0_, f32[24,128,128]{2,1,0:T(8,128)} %refs_1_.1, ...), custom_call_target="tpu_custom_call" | custom-call | tf_op jit(solution)/shard_map/blocks/pallas_call | solution.py:1817
where the time goes:
time: 419 us; the launch traced here: 414 us
  Pallas kernels  413 us (99%)
    pallas_call x1, Pallas kernels, run_scatter(): pl.pallas_call(functools.partial(scatter_kernel, ng=ng, nd=nd, rate=rate)...  116 us
    pallas_call x1, Pallas kernels, run_gather(): pl.pallas_call(functools.partial(gather_kernel, ng=ng, nd=nd), out_shape=...  106 us
    pallas_call x1, Pallas kernels, run_attn_bwd(): pl.pallas_call(functools.partial(attn_bwd_kernel, hpd=hpd, nd=nb), out_sh...  65.7 us
    pallas_call x1, Pallas kernels, run_attn_fwd(): pl.pallas_call(functools.partial(attn_fwd_kernel, hpd=hpd, nd=nb), out_sh...  50.6 us
    pallas_call x1, Pallas kernels, run_mlp(): pl.pallas_call(functools.partial(mlp_kernel, nd=nd, first_o=first_o, firs...  48.7 us
    pallas_call x1, Pallas kernels, run_blocks(): pl.pallas_call(functools.partial(blocks_kernel, handed=len(passing)), gri...  8.62 us
    pallas_call x1, Pallas kernels, run_wgrad(): pl.pallas_call(functools.partial(wgrad_kernel, side=side, tile=tile), out...  8.57 us

commit v1 on v0

--- a/solution.py
+++ b/solution.py
@@ -19,7 +19,6 @@
 highest = lax.Precision.HIGHEST
 F32 = jnp.float32
 BF16 = jnp.bfloat16
-LOG2E = 1.4426950408889634
 MIB = 1024 * 1024
 
 GAIN1, SHIFT1, BQ, BV, BO, GAIN2, SHIFT2, BDOWN, BUP = range(9)
@@ -251,7 +250,7 @@
     _, tok, _ = qbase.shape
     u = lax.broadcasted_iota(jnp.int32, (tok, 128), 0).astype(F32)
     for h in range(hpd):
-        slope = slope_ref[h] * LOG2E
+        slope = slope_ref[h]
         base = spare(h, hpd, lanes)
         near = parts3(jnp.full((tok, 128), slope, F32))
         far = parts3(jnp.full((tok, 128), slope * tok, F32))
@@ -267,28 +266,22 @@
     return columns
 
 
+def with_columns(v, h, hpd, columns):
+    tok, lanes = v.shape
+    if hpd > 1:
+        return jnp.where(own_lanes(h, (tok, lanes), hpd, lanes), v, columns).astype(BF16)
+    return jnp.concatenate([v, columns[:, 0:128 - lanes]], axis=1).astype(BF16)
+
+
 def q_columns(q, h, hpd, columns, extra):
-    tok, lanes = q.shape
-    scaled = q.astype(F32) * ((lanes // hpd) ** (-0.5) * LOG2E)
-    hi = scaled.astype(BF16).astype(F32)
-    low = scaled - hi
+    lanes = q.shape[1]
     if extra:
         columns = extra_lanes(columns, extra, h, hpd, lanes)
-    if hpd > 1:
-        own = own_lanes(h, (tok, lanes), hpd, lanes)
-        return jnp.concatenate(
-            [jnp.where(own, hi, 0.0), jnp.where(own, low, columns)], axis=1
-        ).astype(BF16)
-    return jnp.concatenate([hi, low, columns], axis=1).astype(BF16)
+    return with_columns(q.astype(F32) * ((lanes // hpd) ** (-0.5)), h, hpd, columns)
 
 
 def k_columns(k, h, hpd, columns):
-    tok, lanes = k.shape
-    wide = k.astype(F32)
-    if hpd > 1:
-        own = own_lanes(h, (tok, lanes), hpd, lanes)
-        return jnp.concatenate([wide, jnp.where(own, wide, columns)], axis=1).astype(BF16)
-    return jnp.concatenate([wide, wide, columns], axis=1).astype(BF16)
+    return with_columns(k.astype(F32), h, hpd, columns)
 
 
 def far_side(slope, tok):
@@ -312,12 +305,11 @@
 
 def attn_fwd_kernel(
     span_ref, slope_ref, src, got_out, o_got, o32_out, lse_out,
-    got, o32_ref, lse_ref, sem_w, qa, ka, vt, scores, weights, tops_ref, corr, qbase, kbase, kfar, o_out, ss, sr, os, orr, loc, *, hpd, nd
+    got, o32_ref, lse_ref, sem_w, qa, ka, vt, scores, tops_ref, corr, qbase, kbase, kfar, o_out, ss, sr, os, orr, loc, *, hpd, nd
 ):
     nb, _, seqs, tok, lanes = got.shape
     size = lanes // hpd
     pair = 2 * tok
-    strip = 32
     g = lax.axis_index("grp")
     d = lax.axis_index("dev")
 
@@ -356,7 +348,7 @@
 
     column_tables(slope_ref, qbase, kbase, kfar, hpd, lanes)
     for h in range(hpd):
-        mask, span = far_side(slope_ref[h] * LOG2E, tok)
+        mask, span = far_side(slope_ref[h], tok)
         pair_tables(corr, h, mask, span)
 
     def fold(v, how):
@@ -383,16 +375,12 @@
             for h in range(hpd):
                 top = None
                 for n in range(i + 1):
-                    at = tile_at(i, n)
-                    scores[h, at] = dot_nt(ka[h, n * pair:(n + 1) * pair, :], qa[h, at_i, :])
-                    for r in range(0, pair, strip):
-                        rows = slice(r, r + strip)
-                        v = scores[h, at, rows, :]
-                        if n == i:
-                            v = v + corr[h, flag, rows, :]
-                            scores[h, at, rows, :] = v
-                        here = fold(v, jnp.max)
-                        top = here if top is None else jnp.maximum(top, here)
+                    s = dot_nt(ka[h, n * pair:(n + 1) * pair, :], qa[h, at_i, :])
+                    if n == i:
+                        s = s + corr[h, flag]
+                    scores[h, tile_at(i, n)] = s
+                    here = fold(s, jnp.max)
+                    top = here if top is None else jnp.maximum(top, here)
                 tops_ref[h, i] = jnp.broadcast_to(jnp.max(top, axis=0, keepdims=True), (8, pair))
 
         have(q, 0)
@@ -433,18 +421,14 @@
                 acc = total = None
                 top = tops_ref[h, i][0:1]
                 for n in range(i + 1):
-                    at = tile_at(i, n)
-                    for r in range(0, pair, strip):
-                        rows = slice(r, r + strip)
-                        p = jnp.exp2(scores[h, at, rows, :] - top)
-                        here = fold(p, jnp.sum)
-                        total = here if total is None else total + here
-                        weights[h, n % 2, rows, :] = p.astype(BF16)
-                    part = dot_nn(vt[h * size:(h + 1) * size, n * pair:(n + 1) * pair], weights[h, n % 2])
+                    p = jnp.exp(scores[h, tile_at(i, n)] - top)
+                    here = fold(p, jnp.sum)
+                    part = dot_nn(vt[h * size:(h + 1) * size, n * pair:(n + 1) * pair], p.astype(BF16))
+                    total = here if total is None else total + here
                     acc = part if acc is None else acc + part
                 total = jnp.sum(total, axis=0, keepdims=True)
                 outs.append(acc / total)
-                logs.append(jnp.broadcast_to(top + jnp.log2(total), (128 // hpd, pair)))
+                logs.append(jnp.broadcast_to(top + jnp.log(total), (128 // hpd, pair)))
             out = (jnp.concatenate(outs, axis=0) if hpd > 1 else outs[0]).T
             log = (jnp.concatenate(logs[::-1], axis=0) if hpd > 1 else logs[0]).T
             for k in range(2):
@@ -502,11 +486,10 @@
             pltpu.VMEM((nb, seqs, tok, lanes), F32),
             pltpu.VMEM((nb, seqs, tok, 128), F32),
             dma((3, seqs)),
-            pltpu.VMEM((hpd, t, 256), BF16),
-            pltpu.VMEM((hpd, t, 256), BF16),
+            pltpu.VMEM((hpd, t, 128), BF16),
+            pltpu.VMEM((hpd, t, 128), BF16),
             pltpu.VMEM((lanes, t), BF16),
             pltpu.VMEM((hpd, tiles, 2 * tok, 2 * tok), F32),
-            pltpu.VMEM((hpd, 2, 2 * tok, 2 * tok), BF16),
             pltpu.VMEM((hpd, nb // 2, 8, 2 * tok), F32),
             pltpu.VMEM((hpd, 3, 2 * tok, 2 * tok), F32),
             pltpu.VMEM((hpd, tok, 128), F32),
@@ -527,7 +510,7 @@
 def attn_bwd_kernel(
     span_ref, slope_ref, qkv_in, do_src, o32_in, lse_in, got,
     qkv_ref, o32_ref, lse_ref, sem_in, do_got, out, qa, ka, kt, va, qm, da, dm, dqt, corr, qbase, kbase, kfar,
-    s_ref, dp_ref, p_ref, ds_ref, ss, sr, gs, gr, loc, *, hpd, nd
+    ss, sr, gs, gr, loc, *, hpd, nd
 ):
     nb, _, seqs, tok, lanes = qkv_ref.shape
     inputs = [
@@ -540,7 +523,6 @@
     size = lanes // hpd
     unit = size ** (-0.5)
     pair = 2 * tok
-    strip = 32
     g = lax.axis_index("grp")
     d = lax.axis_index("dev")
 
@@ -575,7 +557,7 @@
         return pltpu.make_async_copy(out.at[d, kind, q], place_back(kind, d, q), gs.at[q, kind, 0])
 
     for h in range(hpd):
-        mask, span = far_side(slope_ref[h] * LOG2E, tok)
+        mask, span = far_side(slope_ref[h], tok)
         pair_tables(corr, h, mask, span)
     column_tables(slope_ref, qbase, kbase, kfar, hpd, lanes)
     row = lax.broadcasted_iota(jnp.int32, (lanes, lanes), 0) // size
@@ -646,18 +628,12 @@
             flag = (start == j * pair).astype(jnp.int32) + 2 * (start == j * pair + tok).astype(jnp.int32)
             dk = dv = None
             for h in range(hpd):
-                s_ref[h] = dot_nt(ka[h, at_j, :], qa[h, at_i, :])
-                dp_ref[h] = dot_nt(va[h, at_j, :], da[h, at_i, :])
-                for r in range(0, pair, strip):
-                    rows = slice(r, r + strip)
-                    s = s_ref[h, rows, :]
-                    if i == j:
-                        s = s + corr[h, flag, rows, :]
-                    p = jnp.exp2(s)
-                    p_ref[h, rows, :] = p.astype(BF16)
-                    ds_ref[h, rows, :] = (p * dp_ref[h, rows, :]).astype(BF16)
-                ds = ds_ref[h]
-                dv_h = dot_nn(p_ref[h], dm[h, at_i, :])
+                s = dot_nt(ka[h, at_j, :], qa[h, at_i, :])
+                if i == j:
+                    s = s + corr[h, flag]
+                p = jnp.exp(s)
+                ds = (p * dot_nt(va[h, at_j, :], da[h, at_i, :])).astype(BF16)
+                dv_h = dot_nn(p.astype(BF16), dm[h, at_i, :])
                 dk_h = dot_nn(ds, qm[h, at_i, :])
                 dk = dk_h if dk is None else dk + dk_h
                 dv = dv_h if dv is None else dv + dv_h
@@ -736,8 +712,8 @@
             dma((3,)),
             pltpu.VMEM((nb, seqs, tok, lanes), BF16),
             pltpu.VMEM(qkv.shape, BF16),
-            pltpu.VMEM((hpd, t, 256), BF16),
-            pltpu.VMEM((hpd, t, 256), BF16),
+            pltpu.VMEM((hpd, t, 128), BF16),
+            pltpu.VMEM((hpd, t, 128), BF16),
             pltpu.VMEM((lanes, t), BF16),
             pltpu.VMEM((hpd, t, wide), BF16),
             pltpu.VMEM((hpd, t, lanes), BF16),
@@ -748,10 +724,6 @@
             pltpu.VMEM((hpd, tok, 128), F32),
             pltpu.VMEM((hpd, tok, 128), F32),
             pltpu.VMEM((hpd, tok, 128), F32),
-            pltpu.VMEM((hpd, 2 * tok, 2 * tok), F32),
-            pltpu.VMEM((hpd, 2 * tok, 2 * tok), F32),
-            pltpu.VMEM((hpd, 2 * tok, 2 * tok), BF16),
-            pltpu.VMEM((hpd, 2 * tok, 2 * tok), BF16),
             dma((seqs, nb)),
             dma((seqs, nb)),
             dma((seqs, 3, nb)),
@@ -766,7 +738,7 @@
 def mlp_kernel(
     slot_ref, att_in, x_in, dy_in, vec_ref, gath,
     act_out, dx1_out, do_out, sums_ref, grads,
-    att_ref, x_ref, dy_ref, sem_in, wo, wup, wdn, x1, acc, dh2, h2_ref, h2t, attt, act_ref, z_ref, dg_ref, g_ref, dz_ref, do_ref, stage,
+    att_ref, x_ref, dy_ref, sem_in, wo, wup, wdn, x1, acc, dh2, h2_ref, h2t, attt, gt, act_ref, z_ref, dg_ref, g_ref, dz_ref, do_ref, stage,
     sem_o, sem_t, sem_g, sem_w, *, nd, first_o, first_up, first_dn, tile
 ):
     rows, width = x_ref.shape
@@ -826,10 +798,10 @@
     for r in range(width // 256):
         h2t[r * 256:(r + 1) * 256, :] = turn(h2_ref[:, r * 256:(r + 1) * 256])
 
-    def put(slot, first, res, down, across):
+    def put(slot, first, res, down, across, stride):
         for i in range(down):
             for j in range(across):
-                stage[slot, first + i * across + j] = res[i * side:(i + 1) * side, j * side:(j + 1) * side]
+                stage[slot, first + i * stride + j] = res[i * side:(i + 1) * side, j * side:(j + 1) * side]
 
     def leave(slot, n, block):
         pltpu.make_async_copy(stage.at[slot, n], grads.at[slot_at(slot_ref, block)], sem_g.at[slot]).start()
@@ -884,17 +856,20 @@
             acc[:, c] += dot_nn(g_ref[slot], wdn[at, :, c])
             dh2[:, c] += dot_nt(dz_ref[slot], wup[at, c, :])
 
+        def turn_g(c):
+            gt[c, :] = turn(g_ref[slot, :, c])
+
         def grad_down(k, c):
-            res = dot_nn(turn(g_ref[slot, :, c]), dy_ref[...]).astype(BF16)
-            put(slot, k * per_piece * per, res, per_piece, per)
+            put(slot, k * per_piece, dot_nn(gt[...], dy_ref[:, c]).astype(BF16), cols, per_piece, per)
 
         def grad_up(k, c):
-            res = dot_nn(h2t[c, :], dz_ref[slot]).astype(BF16)
-            put(slot, per * cols + k * per_piece * cols, res, per_piece, cols)
+            first = per * cols + k * per_piece
+            put(slot, first, dot_nn(h2t[...], dz_ref[slot, :, c]).astype(BF16), per, per_piece, cols)
 
         steps = [functools.partial(up, c) for c in pieces(width)]
-        steps += [functools.partial(grad_down, k, c) for k, c in enumerate(pieces(tile))]
-        steps += [functools.partial(grad_up, k, c) for k, c in enumerate(pieces(width))]
+        steps += [functools.partial(grad_up, k, c) for k, c in enumerate(pieces(tile))]
+        steps += [functools.partial(turn_g, c) for c in pieces(tile)]
+        steps += [functools.partial(grad_down, k, c) for k, c in enumerate(pieces(width))]
         return steps
 
     def send_tile(f):
@@ -975,7 +950,7 @@
     half_rows = width // 2
     for half in range(2):
         res = dot_nn(attt[half * half_rows:(half + 1) * half_rows, :], da_ref[...]).astype(BF16)
-        put(half, 0, res, per // 2, per)
+        put(half, 0, res, per // 2, per, per)
 
         for i in range(per // 2):
             for j in range(per):
@@ -1025,6 +1000,7 @@
             bf16_rows,
             turned,
             turned,
+            pltpu.VMEM((tile, rows), BF16),
             bf16_rows,
             pltpu.VMEM((rows, tile), F32),
             pltpu.VMEM((rows, tile), F32),
@@ -1296,7 +1272,7 @@
         for n in range(3):
             plane(n, t).start()
 
-    def sides(t):
+    def over_x_side(t):
         gz = near_order(t, g, ng)
         landed(0, t, over_x)
         plane(3, t).start()
@@ -1304,6 +1280,9 @@
             plane(9, t).start()
             both_ways(gz, lambda up: corner_line(gz, 1, up).start())
         plane(5, t).start()
+
+    def over_y_side(t):
+        gz = near_order(t, g, ng)
         landed(1, t, over_y)
         plane(4, t).start()
         if t == 0:
@@ -1311,31 +1290,48 @@
             both_ways(gz, lambda up: corner_line(gz, 2, up).start())
         plane(6, t).start()
 
-    def corner(t):
-        gz = near_order(t, g, ng)
-        if t == 0:
-            landed(9, t, across)
-            landed(10, t, across)
-            both_ways(gz, lambda up: corner_line(gz, 3, up).start())
-            plane(11, t).start()
-            plane(12, t).start()
+    def first_corner():
+        landed(9, 0, across)
+        landed(10, 0, across)
+        both_ways(g, lambda up: corner_line(g, 3, up).start())
+        plane(11, 0).start()
+        plane(12, 0).start()
+
+    def corner_x(t):
         landed(3, t, across)
         plane(7, t).start()
+
+    def corner_y(t):
         landed(4, t, across)
         plane(8, t).start()
 
-    def far_corner(t):
+    def far_corner(t, c):
         gz = near_order(t, g, ng)
-        for c in range(4):
-            arrived(region(gz, columns[c], flat, nc), cr.at[gz, c])
-            both_ways(gz, lambda up: corner_line(gz, c, up).start())
-            plane(13 + c, t).start()
-
-    plan = [(t, f) for t in range(ng) for f in (0, 1, 2, 3) if t > 0 or f < 3]
-    lag = {0: 0, 1: 1.5, 2: 2.6, 3: 2.2}
-    for t, f in sorted(plan, key=lambda e: e[0] * 1.0 + lag[e[1]]):
-        (column, sides, corner, far_corner)[f](t)
-        if (t, f) == (0, 0):
+        arrived(region(gz, columns[c], flat, nc), cr.at[gz, c])
+        both_ways(gz, lambda up: corner_line(gz, c, up).start())
+        plane(13 + c, t).start()
+
+    plan = [(t, column, (t,)) for t in range(ng)]
+    plan += [(t + 1.5, side, (t,)) for t in range(ng) for side in (over_x_side, over_y_side)]
+    plan += [(t + 2.61, side, (t,)) for t in range(ng) for side in (corner_x, corner_y)]
+    plan += [(t + 2.2, far_corner, (t, c)) for t in range(1, ng) for c in range(4)]
+    plan += [(2.6, first_corner, ())]
+    plan = [(step, args) for _, step, args in sorted(plan, key=lambda e: e[0])]
+    if ng == 4:
+        plan = [
+            (column, (0,)), (column, (1,)), (over_y_side, (0,)), (over_x_side, (0,)),
+            (column, (2,)), (far_corner, (1, 1)), (over_x_side, (1,)), (over_y_side, (1,)),
+            (column, (3,)), (first_corner, ()), (over_y_side, (2,)), (corner_y, (0,)),
+            (far_corner, (2, 1)), (far_corner, (1, 3)), (far_corner, (1, 0)), (corner_y, (1,)),
+            (over_x_side, (2,)), (far_corner, (2, 2)), (far_corner, (1, 2)), (corner_x, (1,)),
+            (far_corner, (3, 3)), (corner_x, (0,)), (far_corner, (2, 3)), (far_corner, (3, 1)),
+            (far_corner, (3, 0)), (over_x_side, (3,)), (over_y_side, (3,)), (far_corner, (2, 0)),
+            (corner_y, (2,)), (far_corner, (3, 2)), (corner_x, (2,)), (corner_y, (3,)),
+            (corner_x, (3,)),
+        ]
+    for n, (step, args) in enumerate(plan):
+        step(*args)
+        if n == 0:
             prepare(x_ref, block_ref, vin_ref, h1_ref, slot_ref, vec_ref)
 
     for t in range(ng):

time: 419 us -> 413 us (0.986)
  Pallas kernels: 413 us -> 407 us
    pallas_call x1, Pallas kernels: 106 us -> 100 us  [run_gather(): pl.pallas_call(functools.partial(gather_kernel, ng=ng, nd=nd), out_shape=...]
where the time goes in v1:
time: 413 us; the launch traced here: 408 us
  Pallas kernels  407 us (99%)
    pallas_call x1, Pallas kernels, run_scatter(): pl.pallas_call(functools.partial(scatter_kernel, ng=ng, nd=nd, rate=rate)...  118 us
    pallas_call x1, Pallas kernels, run_gather(): pl.pallas_call(functools.partial(gather_kernel, ng=ng, nd=nd), out_shape=...  100 us
    pallas_call x1, Pallas kernels, run_attn_bwd(): pl.pallas_call(functools.partial(attn_bwd_kernel, hpd=hpd, nd=nb), out_sh...  63.8 us
    pallas_call x1, Pallas kernels, run_attn_fwd(): pl.pallas_call(functools.partial(attn_fwd_kernel, hpd=hpd, nd=nb), out_sh...  50.5 us
    pallas_call x1, Pallas kernels, run_mlp(): pl.pallas_call(functools.partial(mlp_kernel, nd=nd, first_o=first_o, firs...  48.7 us
    pallas_call x1, Pallas kernels, run_blocks(): pl.pallas_call(functools.partial(blocks_kernel, handed=len(passing)), gri...  8.62 us
    pallas_call x1, Pallas kernels, run_wgrad(): pl.pallas_call(functools.partial(wgrad_kernel, side=side, tile=tile), out...  8.5 us
    pallas_call x1, Pallas kernels, run_qkv(): pl.pallas_call(functools.partial(qkv_kernel, nd=nd), out_shape=(sds((nd,...  8.31 us

profile of v1, /device:TPU:0, one launch (start us, length us, event | category | flops | bytes accessed | tf_op | source)
XLA Modules:
  0.0 408.4 jit_solution(4854191756944280826)
XLA Ops:
  0.6 0.5 multiply_exponential_fusion.slope_ref
  1.2 100.2 %gather.1 = (bf16[768,128,128]{2,1,0:T(8,128)(2,1)}, bf16[512,1024]{1,0:T(8,128)(2,1)}, s32[6,128]{1,0:T(8,128)}, f32[12,1024]{1,0:T(8,128)}) custom-call(f32[24,128,128]{2,1,0:T(8,128)} %refs_1_.1, bf16[512,1024]{1,0:T(8,128)(2,1)} %bitcast.10, s32[6,128]{1,0:T(8,128)} %bitcast.18, f32[96,128]{1,0:T(8,128)} %bitcast.16), custom_call_target="tpu_custom_call" | custom-call | tf_op jit(solution)/shard_map/gather/pallas_call | solution.py:1355
  101.3 8.3 %qkv.1 = (bf16[8,3,512,128]{3,2,1,0:T(8,128)(2,1)}, bf16[3,1024,1024]{2,1,0:T(8,128)(2,1)}) custom-call(s32[6,128]{1,0:T(8,128)} %get-tuple-element.34.slot_ref, bf16[512,1024]{1,0:T(8,128)(2,1)} %get-tuple-element.35.h1_ref, f32[12,1024]{1,0:T(8,128)} %get-tuple-element.36.vec_ref, bf16[768,128,128]{2,1,0:T(8,128)(2,1)} %get-tuple-element.37.gath), custom_call_target="tpu_custom_call" | custom-call | tf_op jit(solution)/shard_map/qkv/pallas_call | solution.py:165
  109.7 50.5 %attn_fwd.1 = (bf16[8,3,2,256,128]{4,3,2,1,0:T(8,128)(2,1)}, bf16[512,1024]{1,0:T(8,128)(2,1)}, f32[8,2,256,128]{3,2,1,0:T(8,128)}, f32[8,2,256,128]{3,2,1,0:T(8,128)}) custom-call(s32[2]{0:T(128)} %span_ref.3, f32[2]{0:T(128)} %multiply_exponential_fusion.slope_ref, bf16[8,3,2,256,128]{4,3,2,1,0:T(8,128)(2,1)} %bitcast.13), custom_call_target="tpu_custom_call" | custom-call | tf_op jit(solution)/shard_map/attn_fwd/pallas_call | solution.py:474
  160.2 48.7 %mlp.1 = (bf16[512,1024]{1,0:T(8,128)(2,1)}, f32[512,1024]{1,0:T(8,128)}, bf16[8,512,128]{2,1,0:T(8,128)(2,1)}, f32[64,1024]{1,0:T(8,128)}, bf16[768,128,128]{2,1,0:T(8,128)(2,1)}) custom-call(s32[6,128]{1,0:T(8,128)} %get-tuple-element.34.slot_ref, bf16[512,1024]{1,0:T(8,128)(2,1)} %get-tuple-element.39.att_in, bf16[512,1024]{1,0:T(8,128)(2,1)} %bitcast.11, ...), custom_call_target="tpu_custom_call" | custom-call | tf_op jit(solution)/shard_map/mlp/pallas_call | solution.py:976
  208.9 63.8 %attn_bwd.1.cat_ref.cat_in = bf16[512,3072]{1,0:T(8,128)(2,1)} custom-call(s32[2]{0:T(128)} %span_ref.3, f32[2]{0:T(128)} %multiply_exponential_fusion.slope_ref, bf16[8,3,2,256,128]{4,3,2,1,0:T(8,128)(2,1)} %get-tuple-element.41.qkv_in, bf16[8,2,256,128]{3,2,1,0:T(8,128)(2,1)} %bitcast.14, f32[8,2,256,128]{3,2,1,0:T(8,128)} %get-tuple-element.43.o32_in, ...), custom_call_target="tpu_custom_call" | custom-call | tf_op jit(solution)/shard_map/attn_bwd/pallas_call | solution.py:703
  272.7 8.5 %wgrad.1.grads = bf16[768,128,128]{2,1,0:T(8,128)(2,1)} custom-call(s32[6,128]{1,0:T(8,128)} %get-tuple-element.34.slot_ref, bf16[512,1024]{1,0:T(8,128)(2,1)} %get-tuple-element.35.h1_ref, bf16[512,3072]{1,0:T(8,128)(2,1)} %attn_bwd.1.cat_ref.cat_in, bf16[768,128,128]{2,1,0:T(8,128)(2,1)} %get-tuple-element.45.rest), custom_call_target="tpu_custom_call", output_to_operand_aliasing={{}: (3, {})} | custom-call | tf_op jit(solution)/shard_map/wgrad/pallas_call | solution.py:1125
  281.2 118.3 %scatter.1 = (f32[24,128,128]{2,1,0:T(8,128)}, f32[96,128]{1,0:T(8,128)}, f32[96,128]{1,0:T(8,128)}, f32[512,1024]{1,0:T(8,128)}) custom-call(bf16[768,128,128]{2,1,0:T(8,128)(2,1)} %wgrad.1.grads, f32[64,1024]{1,0:T(8,128)} %get-tuple-element.46.sums2_ref, f32[12,1024]{1,0:T(8,128)} %get-tuple-element.36.vec_ref, f32[96,128]{1,0:T(8,128)} %bitcast.17, ...), custom_call_target="tpu_custom_call" | custom-call | tf_op jit(solution)/shard_map/scatter/pallas_call | solution.py:1720
  399.6 8.6 %blocks.1 = (f32[24,128,128]{2,1,0:T(8,128)}, f32[24,128,128]{2,1,0:T(8,128)}, f32[24,128,128]{2,1,0:T(8,128)}, f32[24,128,128]{2,1,0:T(8,128)}, f32[512,1024]{1...) custom-call(f32[24,128,128]{2,1,0:T(8,128)} %get-tuple-element.49.refs_0_, f32[24,128,128]{2,1,0:T(8,128)} %refs_1_.1, ...), custom_call_target="tpu_custom_call" | custom-call | tf_op jit(solution)/shard_map/blocks/pallas_call | solution.py:1813

commit v2 on v1

--- a/solution.py
+++ b/solution.py
@@ -128,7 +128,7 @@
     )(x, blocks, vin)
 
 
-def qkv_kernel(slot_ref, h1_ref, vec_ref, gath, out_ref, wq_out, wbuf, sems, sem_w, *, nd):
+def qkv_kernel(slot_ref, h1_ref, vec_ref, gath, out, wq_out, out_ref, wbuf, sems, sem_w, sem_o, *, nd):
     rows, width = h1_ref.shape
     side = gath.shape[1]
     per = width // side
@@ -138,6 +138,9 @@
             for j in range(per):
                 slot = slot_at(slot_ref, i * 3 * per + part * per + j)
                 fetch_block(gath, slot, wbuf.at[part], i * side, j * side, sems.at[part], side).start()
+
+    def leave(part):
+        return pltpu.make_async_copy(out_ref.at[:, part], out.at[:, part], sem_o.at[part])
 
     def keep(part):
         return pltpu.make_async_copy(wbuf.at[part], wq_out.at[part], sem_w.at[part])
@@ -155,8 +158,10 @@
             res = res.astype(BF16)
             for d in range(nd // 2):
                 out_ref[half * (nd // 2) + d, part, :, :] = res[:, d * lanes:(d + 1) * lanes]
+        leave(part).start()
     for part in range(3):
         keep(part).wait()
+        leave(part).wait()
 
 
 def run_qkv(slot_of, h1, vec, gath, nd):
@@ -166,9 +171,11 @@
         functools.partial(qkv_kernel, nd=nd),
         out_shape=(sds((nd, 3, rows, lanes), BF16), sds((3, width, width), BF16)),
         in_specs=[smem(), vmem(), vmem(), hbm()],
-        out_specs=(vmem(), hbm()),
+        out_specs=(hbm(), hbm()),
         scratch_shapes=[
+            pltpu.VMEM((nd, 3, rows, lanes), BF16),
             pltpu.VMEM((3, width, width), BF16),
+            pltpu.SemaphoreType.DMA((3,)),
             pltpu.SemaphoreType.DMA((3,)),
             pltpu.SemaphoreType.DMA((3,)),
         ],
@@ -1084,12 +1091,23 @@
     )(cat, x, dx1, vec, wq, sums2)
 
 
-def wgrad_kernel(slot_ref, h1_ref, cat_ref, rest, out, a_t, stage, sem_out, *, side, tile):
+def wgrad_kernel(slot_ref, h1_in, cat_in, rest, out, h1_ref, cat_ref, a_t, stage, sem_in, sem_out, *, side, tile):
     del rest
     rows, width = h1_ref.shape
     per = width // side
     cols = tile // side
     steps = cat_ref.shape[1] // tile
+    per_part = width // tile
+    first = pltpu.make_async_copy(h1_in, h1_ref, sem_in.at[0])
+    first.start()
+
+    def part(n):
+        c = slice(n * width, (n + 1) * width)
+        return pltpu.make_async_copy(cat_in.at[:, c], cat_ref.at[:, c], sem_in.at[1 + n])
+
+    for n in range(steps // per_part):
+        part(n).start()
+    first.wait()
     for r in range(width // 256):
         c = slice(r * 256, (r + 1) * 256)
         a_t[c, :] = turn(h1_ref[:, c])
@@ -1097,18 +1115,16 @@
     def left(slot):
         pltpu.make_async_copy(stage.at[slot], stage.at[slot], sem_out.at[slot]).wait()
 
-    @pl.loop(0, steps)
-    def _(t):
-        slot = lax.rem(t, 2)
-
-        @pl.when(t >= 2)
-        def _():
+    for t in range(steps):
+        slot = t % 2
+        if t % per_part == 0:
+            part(t // per_part).wait()
+        if t >= 2:
             left(slot)
-        res = dot_nn(a_t[...], cat_ref[:, pl.ds(pl.multiple_of(t * tile, tile), tile)]).astype(BF16)
+        res = dot_nn(a_t[...], cat_ref[:, t * tile:(t + 1) * tile]).astype(BF16)
         for i in range(per):
             for j in range(cols):
                 stage[slot, i * cols + j] = res[i * side:(i + 1) * side, j * side:(j + 1) * side]
-
         for i in range(per):
             for j in range(cols):
                 dst = slot_at(slot_ref, i * 3 * per + t * cols + j)
@@ -1125,11 +1141,14 @@
     return pl.pallas_call(
         functools.partial(wgrad_kernel, side=side, tile=tile),
         out_shape=sds(grads.shape, BF16),
-        in_specs=[smem(), vmem(), vmem(), hbm()],
+        in_specs=[smem(), hbm(), hbm(), hbm()],
         out_specs=hbm(),
         scratch_shapes=[
+            pltpu.VMEM(h1.shape, BF16),
+            pltpu.VMEM(cat.shape, BF16),
             pltpu.VMEM((width, rows), BF16),
             pltpu.VMEM((2, (width // side) * (tile // side), side, side), BF16),
+            pltpu.SemaphoreType.DMA((4,)),
             pltpu.SemaphoreType.DMA((2,)),
         ],
         input_output_aliases={3: 0},
@@ -1156,6 +1175,15 @@
     low = jnp.where(t < ng - 1 - g, ng - 1 - t, t - (ng - 1 - g))
     high = jnp.where(t < g, t, ng - 1 - (t - g))
     return jnp.where(2 * g < ng, low, high)
+
+
+def far_order(t, g, ng):
+    def low(g):
+        u = t - (ng - 1 - 2 * g)
+        k = g - jnp.maximum(u, 0) // 2
+        return jnp.where(u < 0, ng - 1 - t, jnp.where(u % 2 == 0, g - k, g + k))
+
+    return jnp.where(2 * g < ng, low(g), ng - 1 - low(ng - 1 - g))
 
 
 def greet(g, ng, peers):
@@ -1397,7 +1425,7 @@
         return grads.at[pl.ds((gz * nd + dev) * count, count)]
 
     def order(t):
-        return near_order(ng - 1 - t, g, ng)
+        return far_order(t, g, ng)
 
     for t in range(ng):
         for c in range(4):

time: 413 us -> 404 us (0.978)
  Pallas kernels: 407 us -> 398 us
    pallas_call x1, Pallas kernels: 118 us -> 110 us  [run_scatter(): pl.pallas_call(functools.partial(scatter_kernel, ng=ng, nd=nd, rate=rate)...]
where the time goes in v2:
time: 404 us; the launch traced here: 399 us
  Pallas kernels  398 us (99%)
    pallas_call x1, Pallas kernels, run_scatter(): pl.pallas_call(functools.partial(scatter_kernel, ng=ng, nd=nd, rate=rate)...  110 us
    pallas_call x1, Pallas kernels, run_gather(): pl.pallas_call(functools.partial(gather_kernel, ng=ng, nd=nd), out_shape=...  100 us
    pallas_call x1, Pallas kernels, run_attn_bwd(): pl.pallas_call(functools.partial(attn_bwd_kernel, hpd=hpd, nd=nb), out_sh...  63.8 us
    pallas_call x1, Pallas kernels, run_attn_fwd(): pl.pallas_call(functools.partial(attn_fwd_kernel, hpd=hpd, nd=nb), out_sh...  50.5 us
    pallas_call x1, Pallas kernels, run_mlp(): pl.pallas_call(functools.partial(mlp_kernel, nd=nd, first_o=first_o, firs...  48.7 us
    pallas_call x1, Pallas kernels, run_blocks(): pl.pallas_call(functools.partial(blocks_kernel, handed=len(passing)), gri...  8.62 us
    pallas_call x1, Pallas kernels, run_wgrad(): pl.pallas_call(functools.partial(wgrad_kernel, side=side, tile=tile), out...  8.18 us

profile of v2, /device:TPU:0, one launch (start us, length us, event | category | flops | bytes accessed | tf_op | source)
XLA Modules:
  0.0 399.3 jit_solution(9027117208028464340)
XLA Ops:
  0.6 0.5 multiply_exponential_fusion.slope_ref
  1.2 100.2 %gather.1 = (bf16[768,128,128]{2,1,0:T(8,128)(2,1)}, bf16[512,1024]{1,0:T(8,128)(2,1)}, s32[6,128]{1,0:T(8,128)}, f32[12,1024]{1,0:T(8,128)}) custom-call(f32[24,128,128]{2,1,0:T(8,128)} %refs_1_.1, bf16[512,1024]{1,0:T(8,128)(2,1)} %bitcast.10, s32[6,128]{1,0:T(8,128)} %bitcast.18, f32[96,128]{1,0:T(8,128)} %bitcast.16), custom_call_target="tpu_custom_call" | custom-call | tf_op jit(solution)/shard_map/gather/pallas_call | solution.py:1383
  101.3 7.6 %qkv.1 = (bf16[8,3,512,128]{3,2,1,0:T(8,128)(2,1)}, bf16[3,1024,1024]{2,1,0:T(8,128)(2,1)}) custom-call(s32[6,128]{1,0:T(8,128)} %get-tuple-element.34.slot_ref, bf16[512,1024]{1,0:T(8,128)(2,1)} %get-tuple-element.35.h1_ref.h1_in, f32[12,1024]{1,0:T(8,128)} %get-tuple-element.36.vec_ref, bf16[768,128,128]{2,1,0:T(8,128)(2,1)} %get-tuple-element.37.gath), custom_call_target="tpu_custom_call" | custom-call | tf_op jit(solution)/shard_map/qkv/pallas_call | solution.py:170
  108.9 50.5 %attn_fwd.1 = (bf16[8,3,2,256,128]{4,3,2,1,0:T(8,128)(2,1)}, bf16[512,1024]{1,0:T(8,128)(2,1)}, f32[8,2,256,128]{3,2,1,0:T(8,128)}, f32[8,2,256,128]{3,2,1,0:T(8,128)}) custom-call(s32[2]{0:T(128)} %span_ref.3, f32[2]{0:T(128)} %multiply_exponential_fusion.slope_ref, bf16[8,3,2,256,128]{4,3,2,1,0:T(8,128)(2,1)} %bitcast.13), custom_call_target="tpu_custom_call" | custom-call | tf_op jit(solution)/shard_map/attn_fwd/pallas_call | solution.py:481
  159.4 48.7 %mlp.1 = (bf16[512,1024]{1,0:T(8,128)(2,1)}, f32[512,1024]{1,0:T(8,128)}, bf16[8,512,128]{2,1,0:T(8,128)(2,1)}, f32[64,1024]{1,0:T(8,128)}, bf16[768,128,128]{2,1,0:T(8,128)(2,1)}) custom-call(s32[6,128]{1,0:T(8,128)} %get-tuple-element.34.slot_ref, bf16[512,1024]{1,0:T(8,128)(2,1)} %get-tuple-element.39.att_in, bf16[512,1024]{1,0:T(8,128)(2,1)} %bitcast.11, ...), custom_call_target="tpu_custom_call" | custom-call | tf_op jit(solution)/shard_map/mlp/pallas_call | solution.py:983
  208.2 63.8 %attn_bwd.1.cat_in = bf16[512,3072]{1,0:T(8,128)(2,1)} custom-call(s32[2]{0:T(128)} %span_ref.3, f32[2]{0:T(128)} %multiply_exponential_fusion.slope_ref, bf16[8,3,2,256,128]{4,3,2,1,0:T(8,128)(2,1)} %get-tuple-element.41.qkv_in, bf16[8,2,256,128]{3,2,1,0:T(8,128)(2,1)} %bitcast.14, f32[8,2,256,128]{3,2,1,0:T(8,128)} %get-tuple-element.43.o32_in, ...), custom_call_target="tpu_custom_call" | custom-call | tf_op jit(solution)/shard_map/attn_bwd/pallas_call | solution.py:710
  272.0 8.2 %wgrad.1.grads = bf16[768,128,128]{2,1,0:T(8,128)(2,1)} custom-call(s32[6,128]{1,0:T(8,128)} %get-tuple-element.34.slot_ref, bf16[512,1024]{1,0:T(8,128)(2,1)} %get-tuple-element.35.h1_ref.h1_in, bf16[512,3072]{1,0:T(8,128)(2,1)} %attn_bwd.1.cat_in, bf16[768,128,128]{2,1,0:T(8,128)(2,1)} %get-tuple-element.45.rest), custom_call_target="tpu_custom_call", output_to_operand_aliasing={{}: (3, {})} | custom-call | tf_op jit(solution)/shard_map/wgrad/pallas_call | solution.py:1141
  280.2 110.2 %scatter.1 = (f32[24,128,128]{2,1,0:T(8,128)}, f32[96,128]{1,0:T(8,128)}, f32[96,128]{1,0:T(8,128)}, f32[512,1024]{1,0:T(8,128)}) custom-call(bf16[768,128,128]{2,1,0:T(8,128)(2,1)} %wgrad.1.grads, f32[64,1024]{1,0:T(8,128)} %get-tuple-element.46.sums2_ref, f32[12,1024]{1,0:T(8,128)} %get-tuple-element.36.vec_ref, f32[96,128]{1,0:T(8,128)} %bitcast.17, ...), custom_call_target="tpu_custom_call" | custom-call | tf_op jit(solution)/shard_map/scatter/pallas_call | solution.py:1748
  390.4 8.6 %blocks.1 = (f32[24,128,128]{2,1,0:T(8,128)}, f32[24,128,128]{2,1,0:T(8,128)}, f32[24,128,128]{2,1,0:T(8,128)}, f32[24,128,128]{2,1,0:T(8,128)}, f32[512,1024]{1...) custom-call(f32[24,128,128]{2,1,0:T(8,128)} %get-tuple-element.49.refs_0_, f32[24,128,128]{2,1,0:T(8,128)} %refs_1_.1, ...), custom_call_target="tpu_custom_call" | custom-call | tf_op jit(solution)/shard_map/blocks/pallas_call | solution.py:1841
